TPU v7x, 32 devices: a whole 2x2x4 slice. The times are simulated.
32 devices in a mesh: proj: 8 (over y, x, core), tile: 4 (over z).
Axes of the slice: x: 2, y: 2, z: 4, core: 2. Of those that a mesh axis runs over, the one named last changes fastest.
Arguments:
- raw: bfloat16 [16, 1024, 4096], P(None, 'proj', 'tile'), may hold values from -6 to 6
- row_weights: bfloat16 [16, 4, 128, 256], P('proj', 'tile'), may hold values from 0 to 1
- col_weights: bfloat16 [16, 4, 1024, 2048], P('proj', 'tile'), may hold values from 0 to 1
- band_start: int32 [16, 4], replicated, may hold values from 0 to 768
- band_length: int32 [16, 4], replicated, may hold values from 64 to 256, as said below
- col_offset: int32 [16, 4], P('proj', 'tile'), may hold values from 0 to 24
Outputs:
- slab: float32 [128, 8192], P('proj', 'tile')
Inputs may be any that keep to these rules, and one draw needn't show every extreme that they name: `band_length`: in every projection some tile uses exactly 256 rows.
All inputs are finite; a program needn't handle non-finite values.
Results may differ from a plain program's by a relative error of at most 0.008.
Values may be sent and summed in bfloat16 or wider, within the bound.
A program may use at most 128 MiB of HBM per device.

v0:
```python
import math

import jax
import jax.numpy as jnp
from jax import lax
from jax.sharding import PartitionSpec as P

LMAX = 256


def with_halo(array, sides, width):
    for axis, dim in sides:
        count, length = (lax.axis_size(axis), array.shape[dim])
        up = [(i, (i + 1) % count) for i in range(count - 1)]
        down = [(j, i) for i, j in up]
        last = lax.slice_in_dim(array, length - width, length, axis=dim)
        leading = lax.slice_in_dim(array, 0, width, axis=dim)
        before = lax.ppermute(last, axis, up)
        after = lax.ppermute(leading, axis, down)
        array = jnp.concatenate([before, array, after], axis=dim)
    return array


def tap_tiles():
    rows_a = jnp.arange(128, dtype=jnp.int32)[:, None]
    cols_c = jnp.arange(128, dtype=jnp.int32)[None, :]
    tiles = []
    for shift in (-1, 0, 1):
        offset = cols_c - rows_a - 128 * shift
        offset_f = offset.astype(jnp.float32)
        odd_mask = offset % 2 != 0
        safe_sq = jnp.where(offset == 0, 1.0, offset_f * offset_f)
        value = jnp.where(
            offset == 0, 0.25, jnp.where(odd_mask, -1.0 / (math.pi * math.pi * safe_sq), 0.0)
        )
        value = jnp.where((offset >= -128) & (offset <= 127), value, 0.0)
        tiles.append(value.astype(jnp.bfloat16))
    return tiles


def mask_rows(rows, length):
    mask = jnp.arange(rows.shape[0], dtype=jnp.int32)[:, None] < length
    return jnp.where(mask, rows, jnp.zeros_like(rows))


def take_band(proj_data, start, length):
    return mask_rows(lax.dynamic_slice_in_dim(proj_data, start, LMAX, 0), length)


def body(raw, row_weights, col_weights, band_start, band_length, col_offset):
    proj_count, rows_dev, cols_dev = raw.shape
    n_proj = lax.axis_size("proj")
    n_tile = lax.axis_size("tile")
    proj_me = lax.axis_index("proj")
    tile_me = lax.axis_index("tile")
    total_rows = rows_dev * n_proj
    total_cols = cols_dev * n_tile
    dist = 2.0 * total_cols
    row_ids = (proj_me * rows_dev + jnp.arange(rows_dev, dtype=jnp.int32)).astype(jnp.float32)
    col_ids = (tile_me * cols_dev + jnp.arange(cols_dev, dtype=jnp.int32)).astype(jnp.float32)
    vcoord = row_ids + 0.5 - total_rows / 2.0
    ucoord = col_ids + 0.5 - total_cols / 2.0
    weight = dist / jnp.sqrt(dist * dist + ucoord[None, :] ** 2 + vcoord[:, None] ** 2)
    weighted = (raw.astype(jnp.float32) * weight[None]).astype(jnp.bfloat16)
    padded = with_halo(weighted, (("tile", 2),), 128)
    tiles = tap_tiles()
    blocks = cols_dev // 128
    total = jnp.zeros((proj_count, rows_dev, blocks, 128), jnp.float32)
    for index in range(3):
        piece = padded[:, :, 128 * index : 128 * index + cols_dev].reshape(
            proj_count, rows_dev, blocks, 128
        )
        total = total + jnp.einsum(
            "prna,ab->prnb", piece, tiles[index], preferred_element_type=jnp.float32
        )
    filtered = total.reshape(proj_count, rows_dev, cols_dev).astype(jnp.bfloat16)
    owned = lax.all_to_all(filtered, "proj", split_axis=0, concat_axis=1, tiled=True)
    local_count = owned.shape[0]
    first_proj = proj_me * local_count
    starts = lax.dynamic_slice_in_dim(band_start, first_proj, local_count, 0)
    lengths = lax.dynamic_slice_in_dim(band_length, first_proj, local_count, 0)
    win_cols = col_weights.shape[2]
    my_offsets = col_offset[:, 0]

    def cut_window(band_rows, offset):
        return lax.dynamic_slice_in_dim(band_rows, offset * 128, win_cols, 1)

    full = lax.all_gather(owned, "tile", axis=2, tiled=True)
    my_starts = lax.dynamic_slice_in_dim(starts, tile_me, 1, 1)[:, 0]
    my_lengths = lax.dynamic_slice_in_dim(lengths, tile_me, 1, 1)[:, 0]
    bands = jax.vmap(take_band)(full, my_starts, my_lengths)
    windows = jax.vmap(cut_window)(bands, my_offsets)
    acc = jnp.zeros((row_weights.shape[2], col_weights.shape[3]), jnp.float32)
    for local in range(local_count):
        spread = jnp.dot(
            windows[local], col_weights[local, 0], preferred_element_type=jnp.float32
        ).astype(jnp.bfloat16)
        acc = acc + jnp.dot(row_weights[local, 0], spread, preferred_element_type=jnp.float32)
    return lax.psum_scatter(acc, "proj", scatter_dimension=0, tiled=True)


def solution(mesh):
    return jax.shard_map(
        body,
        mesh=mesh,
        in_specs=(
            P(None, "proj", "tile"),
            P("proj", "tile", None, None),
            P("proj", "tile", None, None),
            P(),
            P(),
            P("proj", "tile"),
        ),
        out_specs=P("proj", "tile"),
        check_vma=False,
    )
```

profile of v0, /device:TPU:0, one launch (start us, length us, event | category | flops | bytes accessed | tf_op | source)
XLA Modules:
  0.0 460.4 jit_solution(14427708411436783929)
XLA Ops:
  6.6 6.4 %copy.20 = bf16[16,128,1024]{1,2,0:T(8,128)(2,1)} copy(bf16[16,128,1024]{2,1,0:T(8,128)(2,1)} %param.6) | data formatting | bytes 8388608 | tf_op args[0]
  13.2 3.4 multiply_convert_fusion
  16.8 5.0 %collective-permute-start = (bf16[16,128,128]{1,2,0:T(8,128)(2,1)S(1)}, bf16[16,128,128]{1,2,0:T(8,128)(2,1)S(1)}, u32[]{:S(2)}, u32[]{:S(2)}) collective-permute-start(bf16[16,128,128]{1,2,0:T(8,128)(2,1)S(1)} %get-tuple-element.44), channel_id=1, source_target_pairs={{0,1},{1,2},{2,3},{4,5},{5,6},{6,7},{8,9},{9,10},{10,11},{12,13},{... | collective-permute-start | bytes 1572872 | tf_op jit(solution)/shard_map/ppermute | solution.py:18
  21.7 1.3 collective-permute-start.1
  23.0 1.3 fusion.57
  24.3 8.6 %collective-permute-done = bf16[16,128,128]{1,2,0:T(8,128)(2,1)S(1)} collective-permute-done((bf16[16,128,128]{1,2,0:T(8,128)(2,1)S(1)}, bf16[16,128,128]{1,2,0:T(8,128)(2,1)S(1)}, u32[]{:S(2)}, u32[]{:S(2)}) %collective-permute-start) | collective-permute-done | bytes 524320 | tf_op jit(solution)/shard_map/ppermute | solution.py:18
  32.9 4.1 collective-permute-done.1
  37.0 2.3 pad_maximum_fusion
  39.3 1.2 fusion.54
  40.5 3.6 add_convert_fusion
  44.1 52.7 %all_to_all.18 = bf16[16,128,1024]{1,2,0:T(8,128)(2,1)} all-to-all(bf16[16,128,1024]{1,2,0:T(8,128)(2,1)S(1)} %bitcast.82), channel_id=1, replica_groups=mesh['proj'=8,'tile'=4] {'proj'}, dimensions={0} | all-to-all | bytes 8388608 | tf_op jit(solution)/shard_map/all_to_all | solution.py:77
  96.8 6.2 %copy.24 = bf16[8,2,128,1024]{3,2,0,1:T(8,128)(2,1)} copy(bf16[8,2,128,1024]{2,3,1,0:T(8,128)(2,1)} %bitcast.80) | data formatting | bytes 8388608 | tf_op jit(solution)/shard_map/all_to_all | solution.py:77
  104.3 284.0 %all-gather.2.cloned.1.call-done = bf16[2,1024,4096]{2,1,0:T(8,128)(2,1)} async-done(((bf16[2,1024,1024]{2,1,0:T(8,128)(2,1)}), bf16[2,1024,4096]{2,1,0:T(8,128)(2,1)}) %all-gather.2.cloned.1.call-update) | async-done | bytes 16777232 | tf_op jit(solution)/shard_map/all_gather | solution.py:88
  388.3 10.9 %while.4 = (s32[]{:T(128)}, bf16[2,1024,4096]{2,1,0:T(8,128)(2,1)}, s32[2,3]{1,0:T(2,128)S(1)}, bf16[2,256,4096]{2,1,0:T(8,128)(2,1)}) while((s32[]{:T(128)}, bf16[2,1024,4096]{2,1,0:T(8,128)(2,1)}, s32[2,3]{1,0:T(2,128)S(1)}, bf16[2,256,4096]{2,1,0:T(8,128)(2,1)}) %tuple.45), condition=%wide.while_cond.clone, body=%wide.while_body.sunk.clone | while | flops 2 | bytes 4195937 | solution.py:47
  389.0 4.8 %dynamic-slice_dynamic-update-slice_fusion.6 = bf16[2,256,4096]{2,1,0:T(8,128)(2,1)} fusion(bf16[2,256,4096]{2,1,0:T(8,128)(2,1)} %get-tuple-element.138, s32[]{:T(128)} %get-tuple-element.135, bf16[2,1024,4096]{2,1,0:T(8,128)(2,1)} %get-tuple-element.140, s32[]{:T(128)} %bitcast.73, s32[]{:T(128)} %bitcast.74), kind=kLoop, calls=%fused_computation.clone.1.clone | loop fusion | bytes 4195840 | tf_op jit(solution)/shard_map/vmap()/gather
  394.4 4.8 %dynamic-slice_dynamic-update-slice_fusion.6 = bf16[2,256,4096]{2,1,0:T(8,128)(2,1)} fusion(bf16[2,256,4096]{2,1,0:T(8,128)(2,1)} %get-tuple-element.138, s32[]{:T(128)} %get-tuple-element.135, bf16[2,1024,4096]{2,1,0:T(8,128)(2,1)} %get-tuple-element.140, s32[]{:T(128)} %bitcast.73, s32[]{:T(128)} %bitcast.74), kind=kLoop, calls=%fused_computation.clone.1.clone | loop fusion | bytes 4195840 | tf_op jit(solution)/shard_map/vmap()/gather
  399.2 4.5 broadcast_select_fusion
  403.7 6.6 %while.5 = (s32[]{:T(128)}, bf16[2,256,4096]{2,1,0:T(8,128)(2,1)}, s32[2,3]{1,0:T(2,128)S(1)}, bf16[2,256,1024]{2,1,0:T(8,128)(2,1)S(1)}) while((s32[]{:T(128)}, bf16[2,256,4096]{2,1,0:T(8,128)(2,1)}, s32[2,3]{1,0:T(2,128)S(1)}, bf16[2,256,1024]{2,1,0:T(8,128)(2,1)S(1)}) %tuple.48), condition=%wide.while_cond.1.clone, body=%wide.while_body.1.sunk.clone | while | flops 2 | bytes 1048685 | solution.py:86
  404.4 2.6 dynamic-slice_dynamic-update-slice_fusion.7
  407.7 2.6 dynamic-slice_dynamic-update-slice_fusion.7
  410.3 3.8 fusion.14
  414.1 3.8 fusion.12
  417.9 1.3 copy.34
  419.2 34.4 %reduce-scatter.4.cloned.1.call-done = f32[16,2048]{1,0:T(8,128)} async-done(((f32[128,2048]{1,0:T(8,128)}), f32[16,2048]{1,0:T(8,128)}) %reduce-scatter.4.cloned.1.call-update) | async-done | bytes 131088 | tf_op jit(solution)/shard_map/reduce_scatter | solution.py:99
  (32 shorter events, 4.2 us)
Async XLA Ops:
  6.5 97.6 %copy-start = (s32[16,4]{0,1:T(4,128)S(1)}, s32[16,4]{0,1:T(4,128)}, u32[]{:S(2)}) copy-start(s32[16,4]{0,1:T(4,128)} %param.10) | copy-start | bytes 772
  6.5 381.8 %all-gather.2.cloned.1.call-start = ((), (), s32[]{:S(2)}) async-start(), calls=%async_computation.2 | async-start | bytes 20971520 | tf_op jit(solution)/shard_map/all_gather | solution.py:88
  16.8 16.1 %collective-permute-start = (bf16[16,128,128]{1,2,0:T(8,128)(2,1)S(1)}, bf16[16,128,128]{1,2,0:T(8,128)(2,1)S(1)}, u32[]{:S(2)}, u32[]{:S(2)}) collective-permute-start(bf16[16,128,128]{1,2,0:T(8,128)(2,1)S(1)} %get-tuple-element.44), channel_id=1, source_target_pairs={{0,1},{1,2},{2,3},{4,5},{5,6},{6,7},{8,9},{9,10},{10,11},{12,13},{... | collective-permute-start | bytes 1572872 | tf_op jit(solution)/shard_map/ppermute | solution.py:18
  21.7 15.3 %collective-permute-start.1 = (bf16[16,128,128]{1,2,0:T(8,128)(2,1)S(1)}, bf16[16,128,128]{1,2,0:T(8,128)(2,1)S(1)}, u32[]{:S(2)}, u32[]{:S(2)}) collective-permute-start(bf16[16,128,128]{1,2,0:T(8,128)(2,1)S(1)} %get-tuple-element.43), channel_id=1, source_target_pairs={{1,0},{2,1},{3,2},{5,4},{6,5},{7,6},{9,8},{10,9},{11,10},{13,12},{... | collective-permute-start | bytes 1572872 | tf_op jit(solution)/shard_map/ppermute | solution.py:19
  103.0 1.0 copy-start.2
  103.1 350.5 %reduce-scatter.4.cloned.1.call-start = ((), (), s32[]{:S(2)}) async-start(), calls=%async_computation.3 | async-start | bytes 1179648 | tf_op jit(solution)/shard_map/reduce_scatter | solution.py:99
  403.7 6.6 %copy-start.1 = (bf16[2,1,128,256]{3,2,1,0:T(8,128)(2,1)S(1)}, bf16[2,1,128,256]{3,2,1,0:T(8,128)(2,1)}, u32[]{:S(2)}) copy-start(bf16[2,1,128,256]{3,2,1,0:T(8,128)(2,1)} %param.7) | copy-start | bytes 393220
Sparse Core Ops, SparseCore 0:
  103.2 285.0 all-gather.1
  419.3 34.2 reduce-scatter.3
where the time goes:
time: 461 us; the launch traced here: 460 us
  waiting for transfers between devices  331 us (72%)
  blocking collectives  52.7 us (11%)
  local copies, waits for them, and re-layouts  32.5 us (7%)
  matrix products  13.7 us (3%)
  between operations  13.5 us (3%)
  other arithmetic  10.6 us (2%)
  starting transfers between devices  6.3 us (1%)
    all_gather x1, waiting for transfers between devices, body(): full = lax.all_gather(owned, 'tile', axis=2, tiled=True)  284 us
    all_to_all x1, blocking collectives, body(): lax.all_to_all(filtered, 'proj', split_axis=0, concat_axis=1, tiled=True)  52.7 us
    reduce_scatter x1, waiting for transfers between devices, body(): return lax.psum_scatter(acc, 'proj', scatter_dimension=0, tiled=True)  34.4 us
    gather x12, local copies, waits for them, and re-layouts  17.4 us
  transfers between devices with their start and end apart: 4, of which 4 were waited for; matrix products, arithmetic and copies ran while one was open for 1% of the time, Pallas kernels for 0%

commit v1 on v0

v1 whole, which is shorter than its diff:
```python
import math

import jax
import jax.numpy as jnp
from jax import lax
from jax.sharding import PartitionSpec as P


def tap_tiles():
    rows_a = jnp.arange(128, dtype=jnp.int32)[:, None]
    cols_c = jnp.arange(128, dtype=jnp.int32)[None, :]
    tiles = []
    for shift in (-1, 0, 1):
        offset = cols_c - rows_a - 128 * shift
        offset_f = offset.astype(jnp.float32)
        odd_mask = offset % 2 != 0
        safe_sq = jnp.where(offset == 0, 1.0, offset_f * offset_f)
        value = jnp.where(
            offset == 0, 0.25, jnp.where(odd_mask, -1.0 / (math.pi * math.pi * safe_sq), 0.0)
        )
        value = jnp.where((offset >= -128) & (offset <= 127), value, 0.0)
        tiles.append(value.astype(jnp.bfloat16))
    return tiles


def banded_rows(weights, starts, lengths, total_rows):
    lmax = weights.shape[-1]
    keep = jnp.arange(lmax, dtype=jnp.int32) < lengths[..., None]
    weights = jnp.where(keep[:, :, None, :], weights, jnp.zeros_like(weights))

    def place(w, start):
        wide = jnp.zeros((w.shape[0], total_rows), w.dtype)
        return lax.dynamic_update_slice(wide, w, (0, start))

    return jax.vmap(jax.vmap(place))(weights, starts)


def body(raw, row_weights, col_weights, band_start, band_length, col_offset):
    proj_count, rows_dev, cols_dev = raw.shape
    n_proj = lax.axis_size("proj")
    n_tile = lax.axis_size("tile")
    proj_me = lax.axis_index("proj")
    tile_me = lax.axis_index("tile")
    total_rows = rows_dev * n_proj
    total_cols = cols_dev * n_tile
    local_count = proj_count // n_proj
    slices = row_weights.shape[2]
    win_cols = col_weights.shape[2]
    dist = 2.0 * total_cols

    first_proj = proj_me * local_count
    starts = lax.dynamic_slice_in_dim(band_start, first_proj, local_count, 0)
    lengths = lax.dynamic_slice_in_dim(band_length, first_proj, local_count, 0)
    all_rw = lax.all_gather(row_weights, "tile", axis=1, tiled=True)
    wide = banded_rows(all_rw, starts, lengths, total_rows)
    wide = wide.reshape(local_count, n_tile * slices, total_rows)

    owned = lax.all_to_all(raw, "proj", split_axis=0, concat_axis=1, tiled=True)
    row_ids = jnp.arange(total_rows, dtype=jnp.int32).astype(jnp.float32)
    col_ids = (tile_me * cols_dev + jnp.arange(cols_dev, dtype=jnp.int32)).astype(jnp.float32)
    vcoord = row_ids + 0.5 - total_rows / 2.0
    ucoord = col_ids + 0.5 - total_cols / 2.0
    weight = dist / jnp.sqrt(dist * dist + ucoord[None, :] ** 2 + vcoord[:, None] ** 2)
    weighted = (owned.astype(jnp.float32) * weight[None]).astype(jnp.bfloat16)

    mixed = jnp.einsum("psr,prc->psc", wide, weighted, preferred_element_type=jnp.float32)
    mixed = mixed.astype(jnp.bfloat16).reshape(local_count, n_tile, slices, cols_dev)
    mine = lax.all_to_all(mixed, "tile", split_axis=1, concat_axis=3, tiled=True)
    mine = jnp.pad(mine[:, 0], ((0, 0), (0, 0), (128, 128)))
    blocks = win_cols // 128
    tiles = tap_tiles()
    windows = []
    for local in range(local_count):
        part = lax.dynamic_slice_in_dim(
            mine[local], 128 * col_offset[local, 0], win_cols + 256, 1
        )
        total = jnp.zeros((slices, blocks, 128), jnp.float32)
        for index in range(3):
            piece = part[:, 128 * index : 128 * index + win_cols].reshape(slices, blocks, 128)
            total = total + jnp.einsum(
                "rna,ab->rnb", piece, tiles[index], preferred_element_type=jnp.float32
            )
        windows.append(total.reshape(slices, win_cols).astype(jnp.bfloat16))
    acc = jnp.zeros((slices, col_weights.shape[3]), jnp.float32)
    for local in range(local_count):
        acc = acc + jnp.dot(
            windows[local], col_weights[local, 0], preferred_element_type=jnp.float32
        )
    parts = acc.astype(jnp.bfloat16).reshape(n_proj, slices // n_proj, -1)
    parts = lax.all_to_all(parts, "proj", split_axis=0, concat_axis=0, tiled=True)
    return jnp.sum(parts.astype(jnp.float32), axis=0)


def solution(mesh):
    return jax.shard_map(
        body,
        mesh=mesh,
        in_specs=(
            P(None, "proj", "tile"),
            P("proj", "tile", None, None),
            P("proj", "tile", None, None),
            P(),
            P(),
            P("proj", "tile"),
        ),
        out_specs=P("proj", "tile"),
        check_vma=False,
    )
```

time: 461 us -> 188 us (0.41)
  waiting for transfers between devices: 331 us -> 44.6 us
  other arithmetic: 10.6 us -> 57.7 us
  blocking collectives: 52.7 us -> 30 us
  between operations: 13.5 us -> 1.52 us
  matrix products: 13.7 us -> 7.96 us
    all_gather x1 -> x0, waiting for transfers between devices: 284 us -> none  [body(): full = lax.all_gather(owned, 'tile', axis=2, tiled=True)]
    scatter x0 -> x17, other arithmetic: none -> 44.6 us
    all_to_all x0 -> x2, waiting for transfers between devices: none -> 44.6 us  [the longest x1 44.6 us: body(): lax.all_to_all(mixed, 'tile', split_axis=1, concat_axis=3, tiled=True)]
    all_to_all x1, blocking collectives: 52.7 us -> 12.8 us  [body(): lax.all_to_all(parts, 'proj', split_axis=0, concat_axis=0, tiled=True)]
    reduce_scatter x1 -> x0, waiting for transfers between devices: 34.4 us -> none  [body(): return lax.psum_scatter(acc, 'proj', scatter_dimension=0, tiled=True)]
    scatter x0 -> x25, local copies, waits for them, and re-layouts: none -> 25.7 us
    gather x12 -> x0, local copies, waits for them, and re-layouts: 17.4 us -> none
    all_gather x0 -> x1, blocking collectives: none -> 17.2 us  [body(): all_rw = lax.all_gather(row_weights, 'tile', axis=1, tiled=True)]
  transfers between devices with their start and end apart: 4 -> 2, of which waited for: 4 -> 1; matrix products, arithmetic and copies ran while one was open for 1% -> 40% of each run, Pallas kernels for 0% -> 0%
where the time goes in v1:
time: 188 us; the launch traced here: 186 us
  other arithmetic  57.7 us (31%)
  waiting for transfers between devices  44.6 us (24%)
  local copies, waits for them, and re-layouts  34.1 us (18%)
  blocking collectives  30 us (16%)
  starting transfers between devices  10.2 us (5%)
  matrix products  7.96 us (4%)
    scatter x16, other arithmetic  44.6 us
    all_to_all x1, waiting for transfers between devices, body(): lax.all_to_all(mixed, 'tile', split_axis=1, concat_axis=3, tiled=True)  44.6 us
    scatter x24, local copies, waits for them, and re-layouts  25.6 us
    all_gather x1, blocking collectives, body(): all_rw = lax.all_gather(row_weights, 'tile', axis=1, tiled=True)  17.2 us
    all_to_all x1, blocking collectives, body(): lax.all_to_all(parts, 'proj', split_axis=0, concat_axis=0, tiled=True)  12.8 us
    convert_element_type x2, other arithmetic, body(): weighted = (owned.astype(jnp.float32) * weight[None]).astype(jnp.bfloat16)  9.45 us
    all_to_all x1, starting transfers between devices, body(): owned = lax.all_to_all(raw, 'proj', split_axis=0, concat_axis=1, tiled=True)  5.32 us
    dot_general x1, matrix products, body(): jnp.einsum('psr,prc->psc', wide, weighted, preferred_element_type=jnp.flo...  5.16 us
  transfers between devices with their start and end apart: 2, of which 1 were waited for; matrix products, arithmetic and copies ran while one was open for 40% of the time, Pallas kernels for 0%

profile of v1, /device:TPU:0, one launch (start us, length us, event | category | flops | bytes accessed | tf_op | source)
XLA Modules:
  0.0 186.3 jit_solution(13444920341885270572)
XLA Ops:
  0.0 5.3 %all-to-all-start = ((bf16[16,128,1024]{2,1,0:T(8,128)(2,1)}), bf16[16,128,1024]{2,1,0:T(8,128)(2,1)}, u32[]{:S(2)}, u32[]{:S(2)}) async-start(bf16[16,128,1024]{2,1,0:T(8,128)(2,1)} %param.6), calls=%async_computation | async-start | bytes 8388608 | tf_op jit(solution)/shard_map/all_to_all | solution.py:58
  5.5 17.2 %all_gather.3 = bf16[2,4,128,256]{3,2,1,0:T(8,128)(2,1)S(1)} all-gather(bf16[2,1,128,256]{3,2,1,0:T(8,128)(2,1)S(1)} %copy-done.1), channel_id=1, replica_groups=mesh['proj'=8,'tile'=4] {'tile'}, dimensions={1}, use_global_device_ids=true | all-gather | bytes 655360 | tf_op jit(solution)/shard_map/all_gather | solution.py:54
  23.0 2.6 %rsqrt_multiply_fusion = f32[1024,1024]{1,0:T(8,128)} fusion(f32[1024]{0:T(1024)S(1)} %get-tuple-element.37, f32[1024]{0:T(1024)S(1)} %get-tuple-element.38), kind=kLoop, calls=%fused_computation.12 | loop fusion | flops 2097152 | bytes 4202496 | tf_op jit(solution)/shard_map/div | solution.py:63
  26.0 70.5 %while.1 = (s32[]{:T(128)}, bf16[2,4,128,1024]{3,2,1,0:T(8,128)(2,1)S(1)}, s32[8,4]{0,1:T(4,128)S(1)}, bf16[8,128,256]{2,1,0:T(8,128)(2,1)S(1)}, s32[]{:T(128)}, /*index=5*/s32[4]{0:T(128)S(1)}, s32[]{:T(128)}) while((s32[]{:T(128)}, bf16[2,4,128,1024]{3,2,1,0:T(8,128)(2,1)S(1)}, s32[8,4]{0,1:T(4,128)S(1)}, bf16[8,128,256]{2,1,0:T(8,128)(2,1)S(1)}, ...), condition=%wide.while_cond, body=%wide.while_body.sunk | while | flops 32797 | bytes 327887 | solution.py:33
  26.6 3.1 %and_reduce_fusion.2 = pred[]{:T(512)} fusion(s32[4]{0:T(128)S(1)} %get-tuple-element.91, s32[1]{0:T(128)} %bitcast.87, s32[1]{0:T(128)} %bitcast.88, s32[1]{0:T(128)} %bitcast.89, s32[1]{0:T(128)} %bitcast.90), kind=kLoop, calls=%fused_computation.1.clone.1 | loop fusion | flops 27 | bytes 33 | tf_op jit(solution)/shard_map/vmap(vmap(vmap()))/scatter
  32.2 2.7 %dynamic-update-slice.3 = bf16[2,4,128,1024]{3,2,1,0:T(8,128)(2,1)S(1)} dynamic-update-slice(bf16[2,4,128,1024]{3,2,1,0:T(8,128)(2,1)S(1)} %get-tuple-element.80, bf16[1,1,128,256]{3,2,1,0:T(8,128)(2,1)S(1)} %bitcast_select_fusion.2, s32[]{:T(128)} %bitcast.84, s32[]{:T(128)} %bitcast.85, s32[]{:T(128)} %constant.67.clone.1..sunk, s32[]{:T(128)} %bitcast.86) | dynamic-update-slice | bytes 131076 | tf_op jit(solution)/shard_map/vmap(vmap(vmap()))/scatter
  35.5 3.1 %and_reduce_fusion.2 = pred[]{:T(512)} fusion(s32[4]{0:T(128)S(1)} %get-tuple-element.91, s32[1]{0:T(128)} %bitcast.87, s32[1]{0:T(128)} %bitcast.88, s32[1]{0:T(128)} %bitcast.89, s32[1]{0:T(128)} %bitcast.90), kind=kLoop, calls=%fused_computation.1.clone.1 | loop fusion | flops 27 | bytes 33 | tf_op jit(solution)/shard_map/vmap(vmap(vmap()))/scatter
  41.1 2.7 %dynamic-update-slice.3 = bf16[2,4,128,1024]{3,2,1,0:T(8,128)(2,1)S(1)} dynamic-update-slice(bf16[2,4,128,1024]{3,2,1,0:T(8,128)(2,1)S(1)} %get-tuple-element.80, bf16[1,1,128,256]{3,2,1,0:T(8,128)(2,1)S(1)} %bitcast_select_fusion.2, s32[]{:T(128)} %bitcast.84, s32[]{:T(128)} %bitcast.85, s32[]{:T(128)} %constant.67.clone.1..sunk, s32[]{:T(128)} %bitcast.86) | dynamic-update-slice | bytes 131076 | tf_op jit(solution)/shard_map/vmap(vmap(vmap()))/scatter
  44.4 3.1 %and_reduce_fusion.2 = pred[]{:T(512)} fusion(s32[4]{0:T(128)S(1)} %get-tuple-element.91, s32[1]{0:T(128)} %bitcast.87, s32[1]{0:T(128)} %bitcast.88, s32[1]{0:T(128)} %bitcast.89, s32[1]{0:T(128)} %bitcast.90), kind=kLoop, calls=%fused_computation.1.clone.1 | loop fusion | flops 27 | bytes 33 | tf_op jit(solution)/shard_map/vmap(vmap(vmap()))/scatter
  50.0 2.7 %dynamic-update-slice.3 = bf16[2,4,128,1024]{3,2,1,0:T(8,128)(2,1)S(1)} dynamic-update-slice(bf16[2,4,128,1024]{3,2,1,0:T(8,128)(2,1)S(1)} %get-tuple-element.80, bf16[1,1,128,256]{3,2,1,0:T(8,128)(2,1)S(1)} %bitcast_select_fusion.2, s32[]{:T(128)} %bitcast.84, s32[]{:T(128)} %bitcast.85, s32[]{:T(128)} %constant.67.clone.1..sunk, s32[]{:T(128)} %bitcast.86) | dynamic-update-slice | bytes 131076 | tf_op jit(solution)/shard_map/vmap(vmap(vmap()))/scatter
  53.3 3.1 %and_reduce_fusion.2 = pred[]{:T(512)} fusion(s32[4]{0:T(128)S(1)} %get-tuple-element.91, s32[1]{0:T(128)} %bitcast.87, s32[1]{0:T(128)} %bitcast.88, s32[1]{0:T(128)} %bitcast.89, s32[1]{0:T(128)} %bitcast.90), kind=kLoop, calls=%fused_computation.1.clone.1 | loop fusion | flops 27 | bytes 33 | tf_op jit(solution)/shard_map/vmap(vmap(vmap()))/scatter
  62.0 3.1 %and_reduce_fusion.2 = pred[]{:T(512)} fusion(s32[4]{0:T(128)S(1)} %get-tuple-element.91, s32[1]{0:T(128)} %bitcast.87, s32[1]{0:T(128)} %bitcast.88, s32[1]{0:T(128)} %bitcast.89, s32[1]{0:T(128)} %bitcast.90), kind=kLoop, calls=%fused_computation.1.clone.1 | loop fusion | flops 27 | bytes 33 | tf_op jit(solution)/shard_map/vmap(vmap(vmap()))/scatter
  70.6 3.1 %and_reduce_fusion.2 = pred[]{:T(512)} fusion(s32[4]{0:T(128)S(1)} %get-tuple-element.91, s32[1]{0:T(128)} %bitcast.87, s32[1]{0:T(128)} %bitcast.88, s32[1]{0:T(128)} %bitcast.89, s32[1]{0:T(128)} %bitcast.90), kind=kLoop, calls=%fused_computation.1.clone.1 | loop fusion | flops 27 | bytes 33 | tf_op jit(solution)/shard_map/vmap(vmap(vmap()))/scatter
  76.2 2.7 %dynamic-update-slice.3 = bf16[2,4,128,1024]{3,2,1,0:T(8,128)(2,1)S(1)} dynamic-update-slice(bf16[2,4,128,1024]{3,2,1,0:T(8,128)(2,1)S(1)} %get-tuple-element.80, bf16[1,1,128,256]{3,2,1,0:T(8,128)(2,1)S(1)} %bitcast_select_fusion.2, s32[]{:T(128)} %bitcast.84, s32[]{:T(128)} %bitcast.85, s32[]{:T(128)} %constant.67.clone.1..sunk, s32[]{:T(128)} %bitcast.86) | dynamic-update-slice | bytes 131076 | tf_op jit(solution)/shard_map/vmap(vmap(vmap()))/scatter
  79.5 3.1 %and_reduce_fusion.2 = pred[]{:T(512)} fusion(s32[4]{0:T(128)S(1)} %get-tuple-element.91, s32[1]{0:T(128)} %bitcast.87, s32[1]{0:T(128)} %bitcast.88, s32[1]{0:T(128)} %bitcast.89, s32[1]{0:T(128)} %bitcast.90), kind=kLoop, calls=%fused_computation.1.clone.1 | loop fusion | flops 27 | bytes 33 | tf_op jit(solution)/shard_map/vmap(vmap(vmap()))/scatter
  88.2 3.1 %and_reduce_fusion.2 = pred[]{:T(512)} fusion(s32[4]{0:T(128)S(1)} %get-tuple-element.91, s32[1]{0:T(128)} %bitcast.87, s32[1]{0:T(128)} %bitcast.88, s32[1]{0:T(128)} %bitcast.89, s32[1]{0:T(128)} %bitcast.90), kind=kLoop, calls=%fused_computation.1.clone.1 | loop fusion | flops 27 | bytes 33 | tf_op jit(solution)/shard_map/vmap(vmap(vmap()))/scatter
  93.8 2.7 %dynamic-update-slice.3 = bf16[2,4,128,1024]{3,2,1,0:T(8,128)(2,1)S(1)} dynamic-update-slice(bf16[2,4,128,1024]{3,2,1,0:T(8,128)(2,1)S(1)} %get-tuple-element.80, bf16[1,1,128,256]{3,2,1,0:T(8,128)(2,1)S(1)} %bitcast_select_fusion.2, s32[]{:T(128)} %bitcast.84, s32[]{:T(128)} %bitcast.85, s32[]{:T(128)} %constant.67.clone.1..sunk, s32[]{:T(128)} %bitcast.86) | dynamic-update-slice | bytes 131076 | tf_op jit(solution)/shard_map/vmap(vmap(vmap()))/scatter
  97.9 3.2 %convert_bitcast_fusion = f32[2,8,128,1024]{3,2,0,1:T(8,128)S(1)} fusion(bf16[8,2,128,1024]{3,2,1,0:T(8,128)(2,1)} %bitcast.36), kind=kLoop, calls=%fused_computation.3 | loop fusion | flops 2097152 | bytes 12582912 | tf_op jit(solution)/shard_map/convert_element_type | solution.py:64
  101.9 6.2 %fusion = bf16[2,1024,1024]{2,1,0:T(8,128)(2,1)} fusion(f32[2,8,128,1024]{3,2,1,0:T(8,128)S(1)} %copy.22, f32[1024,1024]{1,0:T(8,128)} %rsqrt_multiply_fusion), kind=kLoop, calls=%fused_computation.5 | loop fusion | flops 4194304 | bytes 16777216 | tf_op jit(solution)/shard_map/convert_element_type | solution.py:64
  108.2 5.2 %convolution_convert_fusion = bf16[2,512,1024]{2,1,0:T(8,128)(2,1)S(1)} fusion(bf16[2,512,1024]{2,1,0:T(8,128)(2,1)} %bitcast.94, bf16[2,1024,1024]{2,1,0:T(8,128)(2,1)} %fusion), kind=kOutput, calls=%fused_computation.17 | convolution fusion | flops 2148532224 | bytes 8388608 | tf_op jit(solution)/shard_map/psr,prc->psc/dot_general | solution.py:66
  113.3 2.6 %copy.23 = bf16[2,4,128,1024]{2,3,0,1:T(8,128)(2,1)} copy(bf16[2,4,128,1024]{3,2,1,0:T(8,128)(2,1)S(1)} %bitcast.96) | data formatting | bytes 4194304 | tf_op jit(solution)/shard_map/reshape | solution.py:67
  116.0 4.9 %all-to-all-start.1 = ((bf16[2,4,128,1024]{2,3,0,1:T(8,128)(2,1)}), bf16[2,4,128,1024]{2,3,0,1:T(8,128)(2,1)S(1)}, u32[]{:S(2)}, u32[]{:S(2)}) async-start(bf16[2,4,128,1024]{2,3,0,1:T(8,128)(2,1)} %copy.23), calls=%async_computation.1 | async-start | bytes 4194304 | tf_op jit(solution)/shard_map/all_to_all | solution.py:68
  122.8 44.6 %all-to-all-done.1 = bf16[2,4,128,1024]{2,3,0,1:T(8,128)(2,1)S(1)} async-done(((bf16[2,4,128,1024]{2,3,0,1:T(8,128)(2,1)}), bf16[2,4,128,1024]{2,3,0,1:T(8,128)(2,1)S(1)}, u32[]{:S(2)}, u32[]{:S(2)}) %all-to-all-start.1) | async-done | bytes 2097184 | tf_op jit(solution)/shard_map/all_to_all | solution.py:68
  172.8 12.8 %all_to_all.29 = bf16[8,16,2048]{2,1,0:T(8,128)(2,1)S(1)} all-to-all(bf16[8,16,2048]{2,1,0:T(8,128)(2,1)S(1)} %bitcast.95), channel_id=1, replica_groups=mesh['proj'=8,'tile'=4] {'proj'}, dimensions={0} | all-to-all | bytes 1048576 | tf_op jit(solution)/shard_map/all_to_all | solution.py:90
  (75 shorter events, 41.6 us)
Async XLA Ops:
  0.0 5.3 %copy-start.3 = (s32[16,4]{0,1:T(4,128)S(1)}, s32[16,4]{0,1:T(4,128)}, u32[]{:S(2)}) copy-start(s32[16,4]{0,1:T(4,128)} %param.9) | copy-start | bytes 772
  0.0 5.4 %copy-start.4 = (s32[16,4]{0,1:T(4,128)S(1)}, s32[16,4]{0,1:T(4,128)}, u32[]{:S(2)}) copy-start(s32[16,4]{0,1:T(4,128)} %param.10) | copy-start | bytes 772
  0.0 5.5 %copy-start.1 = (bf16[2,1,128,256]{3,2,1,0:T(8,128)(2,1)S(1)}, bf16[2,1,128,256]{3,2,1,0:T(8,128)(2,1)}, u32[]{:S(2)}) copy-start(bf16[2,1,128,256]{3,2,1,0:T(8,128)(2,1)} %param.7) | copy-start | bytes 393220
  0.0 96.5 %all-to-all-start = ((bf16[16,128,1024]{2,1,0:T(8,128)(2,1)}), bf16[16,128,1024]{2,1,0:T(8,128)(2,1)}, u32[]{:S(2)}, u32[]{:S(2)}) async-start(bf16[16,128,1024]{2,1,0:T(8,128)(2,1)} %param.6), calls=%async_computation | async-start | bytes 8388608 | tf_op jit(solution)/shard_map/all_to_all | solution.py:58
  5.3 20.7 %copy-start.2 = (s32[4]{0:T(128)S(1)}, s32[4]{0:T(128)}, u32[]{:S(2)}) copy-start(s32[4]{0:T(128)} %constant.261) | copy-start | bytes 52
  96.5 1.4 copy-start
  113.3 7.6 %copy-start.5 = (s32[2,1]{0,1:T(1,128)S(1)}, s32[2,1]{0,1:T(1,128)}, u32[]{:S(2)}) copy-start(s32[2,1]{0,1:T(1,128)} %param.11) | copy-start | bytes 28
  116.0 51.4 %all-to-all-start.1 = ((bf16[2,4,128,1024]{2,3,0,1:T(8,128)(2,1)}), bf16[2,4,128,1024]{2,3,0,1:T(8,128)(2,1)S(1)}, u32[]{:S(2)}, u32[]{:S(2)}) async-start(bf16[2,4,128,1024]{2,3,0,1:T(8,128)(2,1)} %copy.23), calls=%async_computation.1 | async-start | bytes 4194304 | tf_op jit(solution)/shard_map/all_to_all | solution.py:68
  167.4 2.2 %slice-start = ((s8[8388608]{0:T(1024)(128)(4,1)}), s8[4194304]{0:T(1024)(128)(4,1)S(1)}, s32[]{:S(2)}) async-start(s8[8388608]{0:T(1024)(128)(4,1)} %bitcast.91), calls=%async_computation.3 | async-start | bytes 8388608
  167.5 3.4 %slice-start.1 = ((s8[8388608]{0:T(1024)(128)(4,1)}), s8[4194304]{0:T(1024)(128)(4,1)S(1)}, s32[]{:S(2)}) async-start(s8[8388608]{0:T(1024)(128)(4,1)} %bitcast.91), calls=%async_computation.4 | async-start | bytes 8388608

commit v2 on v1

v2 whole, which is shorter than its diff:
```python
import functools
import math

import jax
import jax.numpy as jnp
import ml_dtypes
import numpy as np
from jax import lax
from jax.experimental import pallas as pl
from jax.experimental.pallas import tpu as pltpu
from jax.sharding import PartitionSpec as P

MESH = pl.DeviceIdType.MESH
CHUNK = 256
PARTS = 2


def tap_matrix():
    n = np.arange(256)[None, :] - np.arange(512)[:, None] + 128
    n_f = np.where(n == 0, 1, n).astype(np.float32)
    odd = -np.float32(1.0) / (np.float32(math.pi * math.pi) * (n_f * n_f))
    value = np.where(n == 0, np.float32(0.25), np.where(n % 2 != 0, odd, np.float32(0.0)))
    value = np.where((n >= -128) & (n <= 127), value, np.float32(0.0))
    return value.astype(ml_dtypes.bfloat16)


def kernel(
    n_proj, n_tile, chunks, cw,
    starts, lengths, offsets, taps, rw, raw, col_w, out,
    landing, wide, weighted, ybuf, zbuf, rwland, filt, cbuf, psend, precv,
    own_sem, raw_send, raw_recv, rw_send, rw_recv, z_send, z_recv, c_sem, p_send, p_recv,
):
    me_p = lax.axis_index("proj")
    me_t = lax.axis_index("tile")
    local_count = landing.shape[1]
    total_rows = landing.shape[2]
    rows_dev = total_rows // n_proj
    cols_dev = chunks * cw
    total_cols = cols_dev * n_tile
    slices, lmax = rw.shape[2], rw.shape[3]
    win_cols = col_w.shape[2]
    vt = col_w.shape[3]
    part_cols = vt // PARTS

    def proj_peer(j):
        return lax.rem(me_p + j, n_proj)

    def proj_source(j):
        return lax.rem(me_p + n_proj - j, n_proj)

    def tile_peer(j):
        return lax.rem(me_t + j, n_tile)

    def tile_source(j):
        return lax.rem(me_t + n_tile - j, n_tile)

    def c_copy(local):
        return pltpu.make_async_copy(
            col_w.at[local, 0], cbuf.at[pl.ds(local * win_cols, win_cols)], c_sem.at[local]
        )

    def own_copy(k):
        return pltpu.make_async_copy(
            raw.at[pl.ds(me_p * local_count, local_count), :, pl.ds(pl.multiple_of(k * cw, cw), cw)],
            landing.at[k, :, pl.ds(pl.multiple_of(me_p * rows_dev, rows_dev), rows_dev)],
            own_sem.at[k],
        )

    def raw_copy(k, j, row_block):
        peer = proj_peer(j)
        return pltpu.make_async_remote_copy(
            src_ref=raw.at[
                pl.ds(peer * local_count, local_count), :, pl.ds(pl.multiple_of(k * cw, cw), cw)
            ],
            dst_ref=landing.at[
                k, :, pl.ds(pl.multiple_of(row_block * rows_dev, rows_dev), rows_dev)
            ],
            send_sem=raw_send.at[k, j],
            recv_sem=raw_recv.at[k, j],
            device_id=(peer, me_t),
            device_id_type=MESH,
        )

    def rw_copy(j, slot):
        return pltpu.make_async_remote_copy(
            src_ref=rw.at[:, 0],
            dst_ref=rwland.at[slot],
            send_sem=rw_send.at[j],
            recv_sem=rw_recv.at[j],
            device_id=(me_p, tile_peer(j)),
            device_id_type=MESH,
        )

    def z_copy(k, j, tile):
        column = pl.multiple_of(128 + tile * cols_dev + k * cw, 128)
        return pltpu.make_async_remote_copy(
            src_ref=ybuf.at[k, tile_peer(j)],
            dst_ref=zbuf.at[:, :, pl.ds(column, cw)],
            send_sem=z_send.at[k, j],
            recv_sem=z_recv.at[k, j],
            device_id=(me_p, tile_peer(j)),
            device_id_type=MESH,
        )

    def p_copy(n, j, slot):
        return pltpu.make_async_remote_copy(
            src_ref=psend.at[n, proj_peer(j)],
            dst_ref=precv.at[n, slot],
            send_sem=p_send.at[n, j],
            recv_sem=p_recv.at[n, j],
            device_id=(proj_peer(j), me_t),
            device_id_type=MESH,
        )

    def each(count, first, f):
        def step(i, carry):
            f(i)
            return carry

        lax.fori_loop(first, count, step, 0)

    barrier = pltpu.get_barrier_semaphore()

    def greet_proj(j):
        pl.semaphore_signal(barrier, inc=1, device_id=(proj_peer(j), me_t), device_id_type=MESH)

    def greet_tile(j):
        pl.semaphore_signal(barrier, inc=1, device_id=(me_p, tile_peer(j)), device_id_type=MESH)

    each(n_proj, 1, greet_proj)
    each(n_tile, 1, greet_tile)
    pl.semaphore_wait(barrier, n_proj + n_tile - 2)

    each(n_tile, 1, lambda j: rw_copy(j, me_t).start())
    for k in range(min(2, chunks)):
        each(n_proj, 1, lambda j: raw_copy(k, j, me_p).start())
    each(chunks, 0, lambda k: own_copy(k).start())
    for local in range(local_count):
        c_copy(local).start()

    edge = jnp.zeros((local_count, slices, 128), zbuf.dtype)
    zbuf[:, :, 0:128] = edge
    zbuf[:, :, 128 + total_cols :] = edge

    rwland[me_t] = rw[:, 0]
    each(n_tile, 1, lambda j: rw_copy(j, tile_source(j)).wait_recv())

    def place(t):
        band_row = lax.broadcasted_iota(jnp.int32, (lmax, total_rows), 0)
        row = lax.broadcasted_iota(jnp.int32, (lmax, total_rows), 1)
        for local in range(local_count):
            start = starts[me_p * local_count + local, t]
            length = lengths[me_p * local_count + local, t]
            hot = (row - band_row == start) & (band_row < length)
            hot = jnp.where(hot, 1.0, 0.0).astype(jnp.bfloat16)
            placed = jnp.dot(rwland[t, local], hot, preferred_element_type=jnp.float32)
            at = pl.ds(pl.multiple_of(t * slices, slices), slices)
            wide[local, at, :] = placed.astype(jnp.bfloat16)

    each(n_tile, 0, place)

    dist = 2.0 * total_cols

    def chunk_step(k):
        each(n_proj, 1, lambda j: raw_copy(k, j, me_p).wait_send())

        @pl.when(k + 2 < chunks)
        def _():
            each(n_proj, 1, lambda j: raw_copy(k + 2, j, me_p).start())

        own_copy(k).wait()
        each(n_proj, 1, lambda j: raw_copy(k, j, proj_source(j)).wait_recv())

        def weigh(b):
            at = pl.ds(pl.multiple_of(b * 128, 128), 128)
            row = b * 128 + lax.broadcasted_iota(jnp.int32, (128, cw), 0)
            column = me_t * cols_dev + k * cw + lax.broadcasted_iota(jnp.int32, (128, cw), 1)
            v = row.astype(jnp.float32) + (0.5 - total_rows / 2.0)
            u = column.astype(jnp.float32) + (0.5 - total_cols / 2.0)
            weight = dist * lax.rsqrt(dist * dist + u * u + v * v)
            for local in range(local_count):
                value = landing[k, local, at, :].astype(jnp.float32) * weight
                weighted[local, at, :] = value.astype(jnp.bfloat16)

        each(total_rows // 128, 0, weigh)

        own_column = pl.multiple_of(128 + me_t * cols_dev + k * cw, 128)

        def mix(t):
            at = pl.ds(pl.multiple_of(t * slices, slices), slices)
            for local in range(local_count):
                y = jnp.dot(
                    wide[local, at, :], weighted[local], preferred_element_type=jnp.float32
                )
                ybuf[k, t, local] = y.astype(jnp.bfloat16)

        each(n_tile, 0, mix)
        each(n_tile, 1, lambda j: z_copy(k, j, me_t).start())
        zbuf[:, :, pl.ds(own_column, cw)] = ybuf[k, me_t]

    each(chunks, 0, chunk_step)

    for local in range(local_count):
        c_copy(local).wait()

    each(n_tile, 1, lambda j: each(chunks, 0, lambda k: z_copy(k, j, tile_source(j)).wait_recv()))

    for local in range(local_count):
        part = zbuf[local]
        bit = 1
        while 2 * bit <= (total_cols - win_cols) // 128:
            bit *= 2
        while bit:
            width = min(win_cols + 256 + 128 * (bit - 1), part.shape[1])
            moved = part[:, 128 * bit : 128 * bit + width]
            if moved.shape[1] < width:
                tail = jnp.zeros((slices, width - moved.shape[1]), part.dtype)
                moved = jnp.concatenate([moved, tail], axis=1)
            skip = jnp.full((slices, width), offsets[local, 0], jnp.int32) & bit
            part = jnp.where(skip != 0, moved, part[:, :width])
            bit //= 2
        for group in range(win_cols // 256):
            value = jnp.dot(
                part[:, 256 * group : 256 * group + 512],
                taps[...],
                preferred_element_type=jnp.float32,
            )
            at = local * win_cols + 256 * group
            filt[:, at : at + 256] = value.astype(jnp.bfloat16)

    for n in range(PARTS):
        for half in range(part_cols // 256):
            at = n * part_cols + 256 * half
            acc = jnp.dot(filt[...], cbuf[:, at : at + 256], preferred_element_type=jnp.float32)
            psend[n, :, :, 256 * half : 256 * half + 256] = acc.reshape(
                n_proj, slices // n_proj, 256
            ).astype(psend.dtype)
        each(n_proj, 1, lambda j: p_copy(n, j, me_p).start())
        precv[n, me_p] = psend[n, me_p]

    for n in range(PARTS):
        each(n_proj, 1, lambda j: p_copy(n, j, proj_source(j)).wait_recv())
        total = precv[n, 0].astype(jnp.float32)
        for source in range(1, n_proj):
            total = total + precv[n, source].astype(jnp.float32)
        out[:, n * part_cols : (n + 1) * part_cols] = total

    each(n_tile, 1, lambda j: rw_copy(j, me_t).wait_send())
    each(n_tile, 1, lambda j: each(chunks, 0, lambda k: z_copy(k, j, me_t).wait_send()))
    for n in range(PARTS):
        each(n_proj, 1, lambda j: p_copy(n, j, me_p).wait_send())


def body(raw, row_weights, col_weights, band_start, band_length, col_offset):
    proj_count, rows_dev, cols_dev = raw.shape
    n_proj = lax.axis_size("proj")
    n_tile = lax.axis_size("tile")
    total_rows = rows_dev * n_proj
    total_cols = cols_dev * n_tile
    local_count, _, slices, lmax = row_weights.shape
    win_cols, vt = col_weights.shape[2:]
    cw = min(CHUNK, cols_dev)
    chunks = cols_dev // cw
    out_rows = slices // n_proj
    sum_type = jnp.bfloat16 if out_rows % 16 == 0 else jnp.float32
    bf16 = jnp.bfloat16
    smem = pl.BlockSpec(memory_space=pltpu.SMEM)
    vmem = pl.BlockSpec(memory_space=pltpu.VMEM)
    hbm = pl.BlockSpec(memory_space=pl.ANY)
    dma = pltpu.SemaphoreType.DMA
    taps = jnp.asarray(tap_matrix())
    flops = 2 * local_count * n_tile * slices * total_rows * cols_dev
    return pl.pallas_call(
        functools.partial(kernel, n_proj, n_tile, chunks, cw),
        out_shape=jax.ShapeDtypeStruct((out_rows, vt), jnp.float32),
        in_specs=[smem, smem, smem, vmem, vmem, hbm, hbm],
        out_specs=vmem,
        scratch_shapes=[
            pltpu.VMEM((chunks, local_count, total_rows, cw), bf16),
            pltpu.VMEM((local_count, n_tile * slices, total_rows), bf16),
            pltpu.VMEM((local_count, total_rows, cw), bf16),
            pltpu.VMEM((chunks, n_tile, local_count, slices, cw), bf16),
            pltpu.VMEM((local_count, slices, total_cols + 256), bf16),
            pltpu.VMEM((n_tile, local_count, slices, lmax), bf16),
            pltpu.VMEM((slices, local_count * win_cols), bf16),
            pltpu.VMEM((local_count * win_cols, vt), bf16),
            pltpu.VMEM((PARTS, n_proj, out_rows, vt // PARTS), sum_type),
            pltpu.VMEM((PARTS, n_proj, out_rows, vt // PARTS), sum_type),
            dma((chunks,)),
            dma((chunks, n_proj)),
            dma((chunks, n_proj)),
            dma((n_tile,)),
            dma((n_tile,)),
            dma((chunks, n_tile)),
            dma((chunks, n_tile)),
            dma((local_count,)),
            dma((PARTS, n_proj)),
            dma((PARTS, n_proj)),
        ],
        compiler_params=pltpu.CompilerParams(
            collective_id=0, has_side_effects=True, vmem_limit_bytes=50 * 1024 * 1024
        ),
        cost_estimate=pl.CostEstimate(
            flops=flops, bytes_accessed=16 * 1024 * 1024, transcendentals=0
        ),
    )(band_start, band_length, col_offset, taps, row_weights, raw, col_weights)


def solution(mesh):
    return jax.shard_map(
        body,
        mesh=mesh,
        in_specs=(
            P(None, "proj", "tile"),
            P("proj", "tile", None, None),
            P("proj", "tile", None, None),
            P(),
            P(),
            P("proj", "tile"),
        ),
        out_specs=P("proj", "tile"),
        check_vma=False,
    )
```

time: 188 us -> 81.7 us (0.43)
  Pallas kernels: 0 us -> 75.4 us
  other arithmetic: 57.7 us -> 0 us
  waiting for transfers between devices: 44.6 us -> 0 us
  blocking collectives: 30 us -> 0 us
  local copies, waits for them, and re-layouts: 34.1 us -> 4.77 us
  starting transfers between devices: 10.2 us -> 0 us
  matrix products: 7.96 us -> 0 us
    pallas_call x0 -> x1, Pallas kernels: none -> 75.4 us  [body(): pl.pallas_call(functools.partial(kernel, n_proj, n_tile, chunks, cw), out...]
    scatter x17 -> x0, other arithmetic: 44.6 us -> none
    all_to_all x2 -> x0, waiting for transfers between devices: 44.6 us -> none  [the longest x1 44.6 us: body(): lax.all_to_all(mixed, 'tile', split_axis=1, concat_axis=3, tiled=True)]
    scatter x25 -> x0, local copies, waits for them, and re-layouts: 25.7 us -> none
    all_gather x1 -> x0, blocking collectives: 17.2 us -> none  [body(): all_rw = lax.all_gather(row_weights, 'tile', axis=1, tiled=True)]
    all_to_all x1 -> x0, blocking collectives: 12.8 us -> none  [body(): lax.all_to_all(parts, 'proj', split_axis=0, concat_axis=0, tiled=True)]
    all_to_all x2 -> x0, starting transfers between devices: 10.2 us -> none  [the longest x1 5.32 us: body(): owned = lax.all_to_all(raw, 'proj', split_axis=0, concat_axis=1, tiled=True)]
    convert_element_type x2 -> x0, other arithmetic: 9.45 us -> none  [body(): weighted = (owned.astype(jnp.float32) * weight[None]).astype(jnp.bfloat16)]
  transfers between devices with their start and end apart: 2 -> 0, of which waited for: 1 -> 0; matrix products, arithmetic and copies ran while one was open for 40% -> 0% of each run, Pallas kernels for 0% -> 0%
where the time goes in v2:
time: 81.7 us; the launch traced here: 80.2 us
  Pallas kernels  75.4 us (92%)
  local copies, waits for them, and re-layouts  4.77 us (6%)
    pallas_call x1, Pallas kernels, body(): pl.pallas_call(functools.partial(kernel, n_proj, n_tile, chunks, cw), out...  75.4 us
    unnamed x8, local copies, waits for them, and re-layouts  4.77 us

profile of v2, /device:TPU:0, one launch (start us, length us, event | category | flops | bytes accessed | tf_op | source)
XLA Modules:
  0.0 80.2 jit_solution(13532345028530217198)
XLA Ops:
  0.0 0.7 copy.10.offsets
  0.7 0.8 copy.8.starts
  1.5 0.8 copy.9.lengths
  2.3 0.0 copy-start
  2.3 0.9 %copy-done = bf16[512,256]{1,0:T(8,128)(2,1)S(1)} copy-done((bf16[512,256]{1,0:T(8,128)(2,1)S(1)}, bf16[512,256]{1,0:T(8,128)(2,1)}, u32[]{:S(2)}) %copy-start) | copy-done | bytes 262168
  3.2 0.0 copy-start.1
  3.2 0.9 %copy-done.1 = bf16[2,1,128,256]{3,2,1,0:T(8,128)(2,1)S(1)} copy-done((bf16[2,1,128,256]{3,2,1,0:T(8,128)(2,1)S(1)}, bf16[2,1,128,256]{3,2,1,0:T(8,128)(2,1)}, u32[]{:S(2)}) %copy-start.1) | copy-done | bytes 131096
  4.1 75.4 %shard_map.73 = f32[16,2048]{1,0:T(8,128)S(1)} custom-call(s32[16,4]{1,0:T(8,128)S(1)} %copy.8.starts, s32[16,4]{1,0:T(8,128)S(1)} %copy.9.lengths, s32[2,1]{1,0:T(2,128)S(1)} %copy.10.offsets, bf16[512,256]{1,0:T(8,128)(2,1)S(1)} %copy-done, bf16[2,1,128,256]{3,2,1,0:T(8,128)(2,1)S(1)} %copy-done.1, bf16[16,128,1024]{2,1,0:T(8,128)(2,1)} %raw.1, ...), custom_call_target="tpu_custom_call" | custom-call | flops 2147483648 | bytes 16777216 | tf_op jit(solution)/shard_map/pallas_call | solution.py:273
  79.6 0.7 copy.12
Async XLA Ops:
  2.3 0.9 %copy-start = (bf16[512,256]{1,0:T(8,128)(2,1)S(1)}, bf16[512,256]{1,0:T(8,128)(2,1)}, u32[]{:S(2)}) copy-start(bf16[512,256]{1,0:T(8,128)(2,1)} %constant.2.clone.taps) | copy-start | bytes 786436
  3.2 0.9 %copy-start.1 = (bf16[2,1,128,256]{3,2,1,0:T(8,128)(2,1)S(1)}, bf16[2,1,128,256]{3,2,1,0:T(8,128)(2,1)}, u32[]{:S(2)}) copy-start(bf16[2,1,128,256]{3,2,1,0:T(8,128)(2,1)} %rw.1) | copy-start | bytes 393220

commit v3 on v2

v3 whole, which is shorter than its diff:
```python
import functools
import math

import jax
import jax.numpy as jnp
import ml_dtypes
import numpy as np
from jax import lax
from jax.experimental import pallas as pl
from jax.experimental.pallas import tpu as pltpu
from jax.sharding import PartitionSpec as P

MESH = pl.DeviceIdType.MESH
CHUNK = 256
PARTS = 4
DEPTH = 3


def tap_matrix():
    n = np.arange(256)[None, :] - np.arange(512)[:, None] + 128
    n_f = np.where(n == 0, 1, n).astype(np.float32)
    odd = -np.float32(1.0) / (np.float32(math.pi * math.pi) * (n_f * n_f))
    value = np.where(n == 0, np.float32(0.25), np.where(n % 2 != 0, odd, np.float32(0.0)))
    value = np.where((n >= -128) & (n <= 127), value, np.float32(0.0))
    return value.astype(ml_dtypes.bfloat16)


def kernel(
    n_proj, n_tile, chunks, cw,
    starts_in, lengths_in, offsets_in, taps_in, rw, raw, col_w, out,
    starts, lengths, offsets, taps,
    landing, wide, weighted, ybuf, zbuf, rwland, filt, cbuf, acc, psend, precv,
    int_sem, tap_sem, own_sem, raw_send, raw_recv, rw_own, rw_send, rw_recv, z_send, z_recv,
    c_sem, p_send, p_recv,
):
    me_p = lax.axis_index("proj")
    me_t = lax.axis_index("tile")
    local_count = landing.shape[1]
    total_rows = landing.shape[2]
    rows_dev = total_rows // n_proj
    cols_dev = chunks * cw
    total_cols = cols_dev * n_tile
    slices, lmax = rw.shape[2], rw.shape[3]
    win_cols = col_w.shape[2]
    vt = col_w.shape[3]
    part_cols = vt // PARTS
    steps = local_count * chunks

    def proj_peer(j):
        return lax.rem(me_p + j, n_proj)

    def proj_source(j):
        return lax.rem(me_p + n_proj - j, n_proj)

    def tile_peer(j):
        return lax.rem(me_t + j, n_tile)

    def tile_source(j):
        return lax.rem(me_t + n_tile - j, n_tile)

    def c_copy(local):
        return pltpu.make_async_copy(col_w.at[local, 0], cbuf.at[local], c_sem.at[local])

    def raw_place(s, row_block):
        rows = pl.ds(pl.multiple_of(row_block * rows_dev, rows_dev), rows_dev)
        return landing.at[lax.rem(s, chunks), lax.div(s, chunks), rows]

    def raw_piece(s, peer):
        columns = pl.ds(pl.multiple_of(lax.rem(s, chunks) * cw, cw), cw)
        return raw.at[peer * local_count + lax.div(s, chunks), :, columns]

    def own_copy(s):
        return pltpu.make_async_copy(raw_piece(s, me_p), raw_place(s, me_p), own_sem.at[s])

    def raw_copy(s, j, row_block):
        peer = proj_peer(j)
        return pltpu.make_async_remote_copy(
            src_ref=raw_piece(s, peer),
            dst_ref=raw_place(s, row_block),
            send_sem=raw_send.at[s, j],
            recv_sem=raw_recv.at[s, j],
            device_id=(peer, me_t),
            device_id_type=MESH,
        )

    def rw_copy(j, slot):
        return pltpu.make_async_remote_copy(
            src_ref=rw.at[:, 0],
            dst_ref=rwland.at[slot],
            send_sem=rw_send.at[j],
            recv_sem=rw_recv.at[j],
            device_id=(me_p, tile_peer(j)),
            device_id_type=MESH,
        )

    def z_place(s, tile):
        column = pl.multiple_of(128 + tile * cols_dev + lax.rem(s, chunks) * cw, 128)
        return zbuf.at[lax.div(s, chunks), :, pl.ds(column, cw)]

    def z_copy(s, j, tile):
        return pltpu.make_async_remote_copy(
            src_ref=ybuf.at[s, tile_peer(j)],
            dst_ref=z_place(s, tile),
            send_sem=z_send.at[s, j],
            recv_sem=z_recv.at[s, j],
            device_id=(me_p, tile_peer(j)),
            device_id_type=MESH,
        )

    def p_copy(n, j, slot):
        return pltpu.make_async_remote_copy(
            src_ref=psend.at[n, proj_peer(j)],
            dst_ref=precv.at[n, slot],
            send_sem=p_send.at[n, j],
            recv_sem=p_recv.at[n, j],
            device_id=(proj_peer(j), me_t),
            device_id_type=MESH,
        )

    def each(count, first, f):
        def step(i, carry):
            f(i)
            return carry

        lax.fori_loop(first, count, step, 0)

    barrier = pltpu.get_barrier_semaphore()

    def greet_proj(j):
        pl.semaphore_signal(barrier, inc=1, device_id=(proj_peer(j), me_t), device_id_type=MESH)

    def greet_tile(j):
        pl.semaphore_signal(barrier, inc=1, device_id=(me_p, tile_peer(j)), device_id_type=MESH)

    each(n_proj, 1, greet_proj)
    each(n_tile, 1, greet_tile)

    small = [
        pltpu.make_async_copy(starts_in, starts, int_sem.at[0]),
        pltpu.make_async_copy(lengths_in, lengths, int_sem.at[1]),
        pltpu.make_async_copy(offsets_in, offsets, int_sem.at[2]),
        pltpu.make_async_copy(rw.at[:, 0], rwland.at[me_t], rw_own),
        pltpu.make_async_copy(taps_in, taps, tap_sem),
    ]
    for copy in small:
        copy.start()
    each(steps, 0, lambda s: own_copy(s).start())
    edge = jnp.zeros((local_count, slices, 128), zbuf.dtype)
    zbuf[:, :, 0:128] = edge
    zbuf[:, :, 128 + total_cols :] = edge

    pl.semaphore_wait(barrier, n_proj + n_tile - 2)

    each(n_tile, 1, lambda j: rw_copy(j, me_t).start())
    for s in range(min(DEPTH, steps)):
        each(n_proj, 1, lambda j: raw_copy(s, j, me_p).start())
    for local in range(local_count):
        c_copy(local).start()
    for copy in small:
        copy.wait()
    each(n_tile, 1, lambda j: rw_copy(j, tile_source(j)).wait_recv())

    def place(local, t):
        band_row = lax.broadcasted_iota(jnp.int32, (lmax, total_rows), 0)
        row = lax.broadcasted_iota(jnp.int32, (lmax, total_rows), 1)
        at = pl.ds(me_p * local_count + local, 1)
        start = starts[at, t : t + 1]
        length = lengths[at, t : t + 1]
        hot = (row - band_row == start) & (band_row < length)
        hot = jnp.where(hot, 1.0, 0.0).astype(jnp.bfloat16)
        placed = jnp.dot(rwland[t, local], hot, preferred_element_type=jnp.float32)
        wide[local, t * slices : (t + 1) * slices, :] = placed.astype(jnp.bfloat16)

    dist = 2.0 * total_cols

    def step(s):
        c, local = lax.rem(s, chunks), lax.div(s, chunks)
        each(n_proj, 1, lambda j: raw_copy(s, j, me_p).wait_send())

        @pl.when(s + DEPTH < steps)
        def _():
            each(n_proj, 1, lambda j: raw_copy(s + DEPTH, j, me_p).start())

        own_copy(s).wait()
        each(n_proj, 1, lambda j: raw_copy(s, j, proj_source(j)).wait_recv())

        def weigh(b):
            at = pl.ds(pl.multiple_of(b * 128, 128), 128)
            row = b * 128 + lax.broadcasted_iota(jnp.int32, (128, cw), 0)
            column = me_t * cols_dev + c * cw + lax.broadcasted_iota(jnp.int32, (128, cw), 1)
            v = row.astype(jnp.float32) + (0.5 - total_rows / 2.0)
            u = column.astype(jnp.float32) + (0.5 - total_cols / 2.0)
            weight = dist * lax.rsqrt(dist * dist + u * u + v * v)
            value = landing[c, local, at, :].astype(jnp.float32) * weight
            weighted[at, :] = value.astype(jnp.bfloat16)

        each(total_rows // 128, 0, weigh)

        def mix(t):
            at = pl.ds(pl.multiple_of(t * slices, slices), slices)
            y = jnp.dot(wide[local, at, :], weighted[...], preferred_element_type=jnp.float32)
            ybuf[s, t] = y.astype(jnp.bfloat16)

        each(n_tile, 0, mix)
        each(n_tile, 1, lambda j: z_copy(s, j, me_t).start())
        column = pl.multiple_of(128 + me_t * cols_dev + c * cw, 128)
        zbuf[local, :, pl.ds(column, cw)] = ybuf[s, me_t]

    def window(local):
        def arrived(s):
            each(n_tile, 1, lambda j: z_copy(s, j, tile_source(j)).wait_recv())

        each((local + 1) * chunks, local * chunks, arrived)
        part = zbuf[local]
        offset = offsets[local : local + 1, :]
        bit = 1
        while 2 * bit <= (total_cols - win_cols) // 128:
            bit *= 2
        while bit:
            width = min(win_cols + 256 + 128 * (bit - 1), part.shape[1])
            moved = part[:, 128 * bit : 128 * bit + width]
            if moved.shape[1] < width:
                tail = jnp.zeros((slices, width - moved.shape[1]), part.dtype)
                moved = jnp.concatenate([moved, tail], axis=1)
            skip = jnp.broadcast_to(offset, (slices, width)) & bit
            part = jnp.where(skip != 0, moved, part[:, :width])
            bit //= 2
        for group in range(win_cols // 256):
            value = jnp.dot(
                part[:, 256 * group : 256 * group + 512],
                taps[...],
                preferred_element_type=jnp.float32,
            )
            filt[local, :, 256 * group : 256 * group + 256] = value.astype(jnp.bfloat16)

    def product(local, at):
        return jnp.dot(
            filt[local], cbuf[local, :, at : at + 256], preferred_element_type=jnp.float32
        )

    def add_up(local):
        window(local)
        c_copy(local).wait()
        for at in range(0, vt, 256):
            value = product(local, at)
            acc[:, at : at + 256] = value if local == 0 else acc[:, at : at + 256] + value

    done = 0
    for local in range(local_count):
        for t in range(n_tile):
            place(local, t)
        if local > 0:
            until = min(local * chunks + 2, steps)
            each(until, done, step)
            done = until
            add_up(local - 1)
        else:
            done = min(chunks - 1, 2)
            each(done, 0, step)
    each(steps, done, step)

    last = local_count - 1
    window(last)
    c_copy(last).wait()
    for n in range(PARTS):
        for half in range(part_cols // 256):
            at = n * part_cols + 256 * half
            value = product(last, at)
            if last > 0:
                value = value + acc[:, at : at + 256]
            psend[n, :, :, 256 * half : 256 * half + 256] = value.reshape(
                n_proj, slices // n_proj, 256
            ).astype(psend.dtype)
        each(n_proj, 1, lambda j: p_copy(n, j, me_p).start())
        precv[n, me_p] = psend[n, me_p]

    for n in range(PARTS):
        each(n_proj, 1, lambda j: p_copy(n, j, proj_source(j)).wait_recv())
        total = precv[n, 0].astype(jnp.float32)
        for source in range(1, n_proj):
            total = total + precv[n, source].astype(jnp.float32)
        out[:, n * part_cols : (n + 1) * part_cols] = total

    each(n_tile, 1, lambda j: rw_copy(j, me_t).wait_send())
    each(n_tile, 1, lambda j: each(steps, 0, lambda s: z_copy(s, j, me_t).wait_send()))
    for n in range(PARTS):
        each(n_proj, 1, lambda j: p_copy(n, j, me_p).wait_send())


def body(raw, row_weights, col_weights, band_start, band_length, col_offset):
    proj_count, rows_dev, cols_dev = raw.shape
    n_proj = lax.axis_size("proj")
    n_tile = lax.axis_size("tile")
    total_rows = rows_dev * n_proj
    total_cols = cols_dev * n_tile
    local_count, _, slices, lmax = row_weights.shape
    win_cols, vt = col_weights.shape[2:]
    cw = min(CHUNK, cols_dev)
    chunks = cols_dev // cw
    steps = local_count * chunks
    out_rows = slices // n_proj
    sum_type = jnp.bfloat16 if out_rows % 16 == 0 else jnp.float32
    bf16 = jnp.bfloat16
    vmem = pl.BlockSpec(memory_space=pltpu.VMEM)
    hbm = pl.BlockSpec(memory_space=pl.ANY)
    dma = pltpu.SemaphoreType.DMA
    taps = jnp.asarray(tap_matrix())
    flops = 2 * local_count * n_tile * slices * total_rows * cols_dev
    return pl.pallas_call(
        functools.partial(kernel, n_proj, n_tile, chunks, cw),
        out_shape=jax.ShapeDtypeStruct((out_rows, vt), jnp.float32),
        in_specs=[hbm] * 7,
        out_specs=vmem,
        scratch_shapes=[
            pltpu.VMEM(band_start.shape, jnp.int32),
            pltpu.VMEM(band_length.shape, jnp.int32),
            pltpu.VMEM(col_offset.shape, jnp.int32),
            pltpu.VMEM(taps.shape, bf16),
            pltpu.VMEM((chunks, local_count, total_rows, cw), bf16),
            pltpu.VMEM((local_count, n_tile * slices, total_rows), bf16),
            pltpu.VMEM((total_rows, cw), bf16),
            pltpu.VMEM((steps, n_tile, slices, cw), bf16),
            pltpu.VMEM((local_count, slices, total_cols + 256), bf16),
            pltpu.VMEM((n_tile, local_count, slices, lmax), bf16),
            pltpu.VMEM((local_count, slices, win_cols), bf16),
            pltpu.VMEM((local_count, win_cols, vt), bf16),
            pltpu.VMEM((slices, vt), jnp.float32),
            pltpu.VMEM((PARTS, n_proj, out_rows, vt // PARTS), sum_type),
            pltpu.VMEM((PARTS, n_proj, out_rows, vt // PARTS), sum_type),
            dma((3,)),
            dma,
            dma((steps,)),
            dma((steps, n_proj)),
            dma((steps, n_proj)),
            dma,
            dma((n_tile,)),
            dma((n_tile,)),
            dma((steps, n_tile)),
            dma((steps, n_tile)),
            dma((local_count,)),
            dma((PARTS, n_proj)),
            dma((PARTS, n_proj)),
        ],
        compiler_params=pltpu.CompilerParams(
            collective_id=0, has_side_effects=True, vmem_limit_bytes=50 * 1024 * 1024
        ),
        cost_estimate=pl.CostEstimate(
            flops=flops, bytes_accessed=16 * 1024 * 1024, transcendentals=0
        ),
    )(band_start, band_length, col_offset, taps, row_weights, raw, col_weights)


def solution(mesh):
    return jax.shard_map(
        body,
        mesh=mesh,
        in_specs=(
            P(None, "proj", "tile"),
            P("proj", "tile", None, None),
            P("proj", "tile", None, None),
            P(),
            P(),
            P("proj", "tile"),
        ),
        out_specs=P("proj", "tile"),
        check_vma=False,
    )
```

time: 81.7 us -> 79.6 us (0.974); the launches traced: 80.2 us -> 79.4 us
  no operation moved by 1% of the time
where the time goes in v3:
time: 79.6 us; the launch traced here: 79.4 us
  Pallas kernels  74.7 us (94%)
  local copies, waits for them, and re-layouts  4.77 us (6%)
    pallas_call x1, Pallas kernels, body(): pl.pallas_call(functools.partial(kernel, n_proj, n_tile, chunks, cw), out...  74.7 us
    unnamed x8, local copies, waits for them, and re-layouts  4.77 us

profile of v3, /device:TPU:0, one launch (start us, length us, event | category | flops | bytes accessed | tf_op | source)
XLA Modules:
  0.0 79.4 jit_solution(2375179574361304857)
XLA Ops:
  0.0 0.7 copy.10.offsets_in
  0.7 0.8 copy.8.starts_in
  1.5 0.8 copy.9.lengths_in
  2.3 0.0 copy-start
  2.3 0.9 %copy-done = bf16[512,256]{1,0:T(8,128)(2,1)S(1)} copy-done((bf16[512,256]{1,0:T(8,128)(2,1)S(1)}, bf16[512,256]{1,0:T(8,128)(2,1)}, u32[]{:S(2)}) %copy-start) | copy-done | bytes 262168
  3.2 0.0 copy-start.1
  3.2 0.9 %copy-done.1 = bf16[2,1,128,256]{3,2,1,0:T(8,128)(2,1)S(1)} copy-done((bf16[2,1,128,256]{3,2,1,0:T(8,128)(2,1)S(1)}, bf16[2,1,128,256]{3,2,1,0:T(8,128)(2,1)}, u32[]{:S(2)}) %copy-start.1) | copy-done | bytes 131096
  4.1 74.7 %shard_map.73 = f32[16,2048]{1,0:T(8,128)S(1)} custom-call(s32[16,4]{1,0:T(8,128)S(1)} %copy.8.starts_in, s32[16,4]{1,0:T(8,128)S(1)} %copy.9.lengths_in, s32[2,1]{1,0:T(2,128)S(1)} %copy.10.offsets_in, bf16[512,256]{1,0:T(8,128)(2,1)S(1)} %copy-done, bf16[2,1,128,256]{3,2,1,0:T(8,128)(2,1)S(1)} %copy-done.1, bf16[16,128,1024]{2,1,0:T(8,128)(2,1)} %raw.1, ...), custom_call_target="tpu_custom_call" | custom-call | flops 2147483648 | bytes 16777216 | tf_op jit(solution)/shard_map/pallas_call | solution.py:309
  78.8 0.7 copy.12
Async XLA Ops:
  2.3 0.9 %copy-start = (bf16[512,256]{1,0:T(8,128)(2,1)S(1)}, bf16[512,256]{1,0:T(8,128)(2,1)}, u32[]{:S(2)}) copy-start(bf16[512,256]{1,0:T(8,128)(2,1)} %constant.2.clone.taps_in) | copy-start | bytes 786436
  3.2 0.9 %copy-start.1 = (bf16[2,1,128,256]{3,2,1,0:T(8,128)(2,1)S(1)}, bf16[2,1,128,256]{3,2,1,0:T(8,128)(2,1)}, u32[]{:S(2)}) copy-start(bf16[2,1,128,256]{3,2,1,0:T(8,128)(2,1)} %rw.1) | copy-start | bytes 393220

commit v4 on v3

--- a/solution.py
+++ b/solution.py
@@ -3,34 +3,35 @@
 
 import jax
 import jax.numpy as jnp
-import ml_dtypes
-import numpy as np
 from jax import lax
 from jax.experimental import pallas as pl
 from jax.experimental.pallas import tpu as pltpu
 from jax.sharding import PartitionSpec as P
 
 MESH = pl.DeviceIdType.MESH
-CHUNK = 256
+CHUNK = 128
 PARTS = 4
-DEPTH = 3
+DEPTH = 6
+VMEM_BYTES = 63 * 1024 * 1024
 
 
 def tap_matrix():
-    n = np.arange(256)[None, :] - np.arange(512)[:, None] + 128
-    n_f = np.where(n == 0, 1, n).astype(np.float32)
-    odd = -np.float32(1.0) / (np.float32(math.pi * math.pi) * (n_f * n_f))
-    value = np.where(n == 0, np.float32(0.25), np.where(n % 2 != 0, odd, np.float32(0.0)))
-    value = np.where((n >= -128) & (n <= 127), value, np.float32(0.0))
-    return value.astype(ml_dtypes.bfloat16)
+    row = lax.broadcasted_iota(jnp.int32, (512, 256), 0)
+    n = lax.broadcasted_iota(jnp.int32, (512, 256), 1) - row + 128
+    n_f = n.astype(jnp.float32)
+    safe_sq = jnp.where(n == 0, 1.0, n_f * n_f)
+    odd = jnp.where((n & 1) != 0, -1.0 / (math.pi * math.pi * safe_sq), 0.0)
+    value = jnp.where(n == 0, 0.25, odd)
+    value = jnp.where((n >= -128) & (n <= 127), value, 0.0)
+    return value.astype(jnp.bfloat16)
 
 
 def kernel(
     n_proj, n_tile, chunks, cw,
-    starts_in, lengths_in, offsets_in, taps_in, rw, raw, col_w, out,
+    starts_in, lengths_in, offsets_in, rw, raw, col_w, out,
     starts, lengths, offsets, taps,
     landing, wide, weighted, ybuf, zbuf, rwland, filt, cbuf, acc, psend, precv,
-    int_sem, tap_sem, own_sem, raw_send, raw_recv, rw_own, rw_send, rw_recv, z_send, z_recv,
+    int_sem, own_sem, raw_send, raw_recv, rw_own, rw_send, rw_recv, z_send, z_recv,
     c_sem, p_send, p_recv,
 ):
     me_p = lax.axis_index("proj")
@@ -47,10 +48,19 @@
     steps = local_count * chunks
 
     def proj_peer(j):
-        return lax.rem(me_p + j, n_proj)
-
-    def proj_source(j):
-        return lax.rem(me_p + n_proj - j, n_proj)
+        mask = mask_of(j)
+        peer, bit = me_p, 1
+        while bit < n_proj:
+            change = lax.rem(lax.div(mask, bit), 2)
+            mine = lax.rem(lax.div(me_p, bit), 2)
+            peer = peer + bit * change * (1 - 2 * mine)
+            bit *= 2
+        return peer
+
+    def mask_of(j):
+        mask = lax.rem(2 * j, n_proj) + lax.div(2 * j, n_proj)
+        one, two = lax.rem(lax.div(mask, 2), 2), lax.rem(lax.div(mask, 4), 2)
+        return mask + 2 * (two - one) * lax.rem(me_p, 2) - 4 * (two - one) * lax.rem(me_p, 2)
 
     def tile_peer(j):
         return lax.rem(me_t + j, n_tile)
@@ -77,8 +87,8 @@
         return pltpu.make_async_remote_copy(
             src_ref=raw_piece(s, peer),
             dst_ref=raw_place(s, row_block),
-            send_sem=raw_send.at[s, j],
-            recv_sem=raw_recv.at[s, j],
+            send_sem=raw_send.at[s, mask_of(j)],
+            recv_sem=raw_recv.at[s, mask_of(j)],
             device_id=(peer, me_t),
             device_id_type=MESH,
         )
@@ -111,8 +121,8 @@
         return pltpu.make_async_remote_copy(
             src_ref=psend.at[n, proj_peer(j)],
             dst_ref=precv.at[n, slot],
-            send_sem=p_send.at[n, j],
-            recv_sem=p_recv.at[n, j],
+            send_sem=p_send.at[n, mask_of(j)],
+            recv_sem=p_recv.at[n, mask_of(j)],
             device_id=(proj_peer(j), me_t),
             device_id_type=MESH,
         )
@@ -140,7 +150,6 @@
         pltpu.make_async_copy(lengths_in, lengths, int_sem.at[1]),
         pltpu.make_async_copy(offsets_in, offsets, int_sem.at[2]),
         pltpu.make_async_copy(rw.at[:, 0], rwland.at[me_t], rw_own),
-        pltpu.make_async_copy(taps_in, taps, tap_sem),
     ]
     for copy in small:
         copy.start()
@@ -156,6 +165,7 @@
         each(n_proj, 1, lambda j: raw_copy(s, j, me_p).start())
     for local in range(local_count):
         c_copy(local).start()
+    taps[...] = tap_matrix()
     for copy in small:
         copy.wait()
     each(n_tile, 1, lambda j: rw_copy(j, tile_source(j)).wait_recv())
@@ -163,9 +173,10 @@
     def place(local, t):
         band_row = lax.broadcasted_iota(jnp.int32, (lmax, total_rows), 0)
         row = lax.broadcasted_iota(jnp.int32, (lmax, total_rows), 1)
-        at = pl.ds(me_p * local_count + local, 1)
-        start = starts[at, t : t + 1]
-        length = lengths[at, t : t + 1]
+        mine = lax.broadcasted_iota(jnp.int32, (1, starts.shape[1]), 1)
+        mine = mine == me_p * local_count + local
+        start = jnp.sum(jnp.where(mine, starts[t : t + 1, :], 0), axis=1, keepdims=True)
+        length = jnp.sum(jnp.where(mine, lengths[t : t + 1, :], 0), axis=1, keepdims=True)
         hot = (row - band_row == start) & (band_row < length)
         hot = jnp.where(hot, 1.0, 0.0).astype(jnp.bfloat16)
         placed = jnp.dot(rwland[t, local], hot, preferred_element_type=jnp.float32)
@@ -182,7 +193,7 @@
             each(n_proj, 1, lambda j: raw_copy(s + DEPTH, j, me_p).start())
 
         own_copy(s).wait()
-        each(n_proj, 1, lambda j: raw_copy(s, j, proj_source(j)).wait_recv())
+        each(n_proj, 1, lambda j: raw_copy(s, j, proj_peer(j)).wait_recv())
 
         def weigh(b):
             at = pl.ds(pl.multiple_of(b * 128, 128), 128)
@@ -196,12 +207,8 @@
 
         each(total_rows // 128, 0, weigh)
 
-        def mix(t):
-            at = pl.ds(pl.multiple_of(t * slices, slices), slices)
-            y = jnp.dot(wide[local, at, :], weighted[...], preferred_element_type=jnp.float32)
-            ybuf[s, t] = y.astype(jnp.bfloat16)
-
-        each(n_tile, 0, mix)
+        y = jnp.dot(wide[local], weighted[...], preferred_element_type=jnp.float32)
+        ybuf[s] = y.astype(jnp.bfloat16).reshape(n_tile, slices, cw)
         each(n_tile, 1, lambda j: z_copy(s, j, me_t).start())
         column = pl.multiple_of(128 + me_t * cols_dev + c * cw, 128)
         zbuf[local, :, pl.ds(column, cw)] = ybuf[s, me_t]
@@ -212,7 +219,7 @@
 
         each((local + 1) * chunks, local * chunks, arrived)
         part = zbuf[local]
-        offset = offsets[local : local + 1, :]
+        offset = offsets[:, local : local + 1]
         bit = 1
         while 2 * bit <= (total_cols - win_cols) // 128:
             bit *= 2
@@ -275,7 +282,7 @@
         precv[n, me_p] = psend[n, me_p]
 
     for n in range(PARTS):
-        each(n_proj, 1, lambda j: p_copy(n, j, proj_source(j)).wait_recv())
+        each(n_proj, 1, lambda j: p_copy(n, j, proj_peer(j)).wait_recv())
         total = precv[n, 0].astype(jnp.float32)
         for source in range(1, n_proj):
             total = total + precv[n, source].astype(jnp.float32)
@@ -304,18 +311,17 @@
     vmem = pl.BlockSpec(memory_space=pltpu.VMEM)
     hbm = pl.BlockSpec(memory_space=pl.ANY)
     dma = pltpu.SemaphoreType.DMA
-    taps = jnp.asarray(tap_matrix())
     flops = 2 * local_count * n_tile * slices * total_rows * cols_dev
     return pl.pallas_call(
         functools.partial(kernel, n_proj, n_tile, chunks, cw),
         out_shape=jax.ShapeDtypeStruct((out_rows, vt), jnp.float32),
-        in_specs=[hbm] * 7,
+        in_specs=[hbm] * 6,
         out_specs=vmem,
         scratch_shapes=[
-            pltpu.VMEM(band_start.shape, jnp.int32),
-            pltpu.VMEM(band_length.shape, jnp.int32),
-            pltpu.VMEM(col_offset.shape, jnp.int32),
-            pltpu.VMEM(taps.shape, bf16),
+            pltpu.VMEM((n_tile, proj_count), jnp.int32),
+            pltpu.VMEM((n_tile, proj_count), jnp.int32),
+            pltpu.VMEM((1, local_count), jnp.int32),
+            pltpu.VMEM((512, 256), bf16),
             pltpu.VMEM((chunks, local_count, total_rows, cw), bf16),
             pltpu.VMEM((local_count, n_tile * slices, total_rows), bf16),
             pltpu.VMEM((total_rows, cw), bf16),
@@ -328,7 +334,6 @@
             pltpu.VMEM((PARTS, n_proj, out_rows, vt // PARTS), sum_type),
             pltpu.VMEM((PARTS, n_proj, out_rows, vt // PARTS), sum_type),
             dma((3,)),
-            dma,
             dma((steps,)),
             dma((steps, n_proj)),
             dma((steps, n_proj)),
@@ -342,12 +347,12 @@
             dma((PARTS, n_proj)),
         ],
         compiler_params=pltpu.CompilerParams(
-            collective_id=0, has_side_effects=True, vmem_limit_bytes=50 * 1024 * 1024
+            collective_id=0, has_side_effects=True, vmem_limit_bytes=VMEM_BYTES
         ),
         cost_estimate=pl.CostEstimate(
             flops=flops, bytes_accessed=16 * 1024 * 1024, transcendentals=0
         ),
-    )(band_start, band_length, col_offset, taps, row_weights, raw, col_weights)
+    )(band_start.T, band_length.T, col_offset.T, row_weights, raw, col_weights)
 
 
 def solution(mesh):

time: 79.6 us -> 80.6 us (1.013)
  Pallas kernels: 74.7 us -> 78.9 us
  local copies, waits for them, and re-layouts: 4.77 us -> 1.57 us
    pallas_call x1, Pallas kernels: 74.7 us -> 78.9 us  [body(): pl.pallas_call(functools.partial(kernel, n_proj, n_tile, chunks, cw), out...]
    unnamed x8 -> x1, local copies, waits for them, and re-layouts: 4.77 us -> 1.57 us
where the time goes in v4:
time: 80.6 us; the launch traced here: 80.5 us
  Pallas kernels  78.9 us (98%)
  local copies, waits for them, and re-layouts  1.57 us (2%)
    pallas_call x1, Pallas kernels, body(): pl.pallas_call(functools.partial(kernel, n_proj, n_tile, chunks, cw), out...  78.9 us

profile of v4, /device:TPU:0, one launch (start us, length us, event | category | flops | bytes accessed | tf_op | source)
XLA Modules:
  0.0 80.5 jit_solution(17468099019266146361)
XLA Ops:
  0.0 78.9 %shard_map.64 = f32[16,2048]{1,0:T(8,128)} custom-call(s32[4,16]{1,0:T(4,128)} %bitcast.3, s32[4,16]{1,0:T(4,128)} %bitcast.4, s32[1,2]{1,0:T(1,128)} %bitcast.5, bf16[2,1,128,256]{3,2,1,0:T(8,128)(2,1)} %rw.1, bf16[16,128,1024]{2,1,0:T(8,128)(2,1)} %raw.1, bf16[2,1,1024,2048]{3,2,1,0:T(8,128)(2,1)} %col_w.1), custom_call_target="tpu_custom_call" | custom-call | flops 2147483648 | bytes 16777216 | tf_op jit(solution)/shard_map/pallas_call | solution.py:315
  78.9 1.6 %copy.8 = f32[16,2048]{1,0:T(8,128)} copy(f32[16,2048]{1,0:T(8,128)} %shard_map.64) | data formatting | bytes 262144

commit v5 on v4

--- a/solution.py
+++ b/solution.py
@@ -9,9 +9,9 @@
 from jax.sharding import PartitionSpec as P
 
 MESH = pl.DeviceIdType.MESH
-CHUNK = 128
+CHUNK = 256
 PARTS = 4
-DEPTH = 6
+DEPTH = 3
 VMEM_BYTES = 63 * 1024 * 1024
 
 
@@ -47,26 +47,30 @@
     part_cols = vt // PARTS
     steps = local_count * chunks
 
+    core = lax.rem(me_p, 2)
+    bits, bit = [], 1
+    while bit < n_proj:
+        bits.append(bit * (1 - 2 * lax.rem(lax.div(me_p, bit), 2)))
+        bit *= 2
+
+    def flipped(mask):
+        return sum(((mask >> i) & 1) * step for i, step in enumerate(bits))
+
+    proj_peers = {}
+    for j in [*range(2, n_proj, 2), *range(n_proj - 1, 0, -2)]:
+        other = (j & ~6) | ((j & 2) << 1) | ((j & 4) >> 1) if j % 2 == 0 and n_proj > 4 else j
+        proj_peers[j] = me_p + flipped(j) + core * (flipped(other) - flipped(j))
+    tile_peers = {j: lax.rem(me_t + j, n_tile) for j in range(1, n_tile)}
+    tile_sources = {j: lax.rem(me_t + n_tile - j, n_tile) for j in range(1, n_tile)}
+
     def proj_peer(j):
-        mask = mask_of(j)
-        peer, bit = me_p, 1
-        while bit < n_proj:
-            change = lax.rem(lax.div(mask, bit), 2)
-            mine = lax.rem(lax.div(me_p, bit), 2)
-            peer = peer + bit * change * (1 - 2 * mine)
-            bit *= 2
-        return peer
-
-    def mask_of(j):
-        mask = lax.rem(2 * j, n_proj) + lax.div(2 * j, n_proj)
-        one, two = lax.rem(lax.div(mask, 2), 2), lax.rem(lax.div(mask, 4), 2)
-        return mask + 2 * (two - one) * lax.rem(me_p, 2) - 4 * (two - one) * lax.rem(me_p, 2)
+        return proj_peers[j]
 
     def tile_peer(j):
-        return lax.rem(me_t + j, n_tile)
+        return tile_peers[j]
 
     def tile_source(j):
-        return lax.rem(me_t + n_tile - j, n_tile)
+        return tile_sources[j]
 
     def c_copy(local):
         return pltpu.make_async_copy(col_w.at[local, 0], cbuf.at[local], c_sem.at[local])
@@ -87,8 +91,8 @@
         return pltpu.make_async_remote_copy(
             src_ref=raw_piece(s, peer),
             dst_ref=raw_place(s, row_block),
-            send_sem=raw_send.at[s, mask_of(j)],
-            recv_sem=raw_recv.at[s, mask_of(j)],
+            send_sem=raw_send.at[s, j],
+            recv_sem=raw_recv.at[s, j],
             device_id=(peer, me_t),
             device_id_type=MESH,
         )
@@ -121,8 +125,8 @@
         return pltpu.make_async_remote_copy(
             src_ref=psend.at[n, proj_peer(j)],
             dst_ref=precv.at[n, slot],
-            send_sem=p_send.at[n, mask_of(j)],
-            recv_sem=p_recv.at[n, mask_of(j)],
+            send_sem=p_send.at[n, j],
+            recv_sem=p_recv.at[n, j],
             device_id=(proj_peer(j), me_t),
             device_id_type=MESH,
         )
@@ -134,6 +138,14 @@
 
         lax.fori_loop(first, count, step, 0)
 
+    def each_proj(f):
+        for j in proj_peers:
+            f(j)
+
+    def each_tile(f):
+        for j in tile_peers:
+            f(j)
+
     barrier = pltpu.get_barrier_semaphore()
 
     def greet_proj(j):
@@ -142,8 +154,8 @@
     def greet_tile(j):
         pl.semaphore_signal(barrier, inc=1, device_id=(me_p, tile_peer(j)), device_id_type=MESH)
 
-    each(n_proj, 1, greet_proj)
-    each(n_tile, 1, greet_tile)
+    each_proj(greet_proj)
+    each_tile(greet_tile)
 
     small = [
         pltpu.make_async_copy(starts_in, starts, int_sem.at[0]),
@@ -160,15 +172,15 @@
 
     pl.semaphore_wait(barrier, n_proj + n_tile - 2)
 
-    each(n_tile, 1, lambda j: rw_copy(j, me_t).start())
+    each_tile(lambda j: rw_copy(j, me_t).start())
     for s in range(min(DEPTH, steps)):
-        each(n_proj, 1, lambda j: raw_copy(s, j, me_p).start())
+        each_proj(lambda j: raw_copy(s, j, me_p).start())
     for local in range(local_count):
         c_copy(local).start()
     taps[...] = tap_matrix()
     for copy in small:
         copy.wait()
-    each(n_tile, 1, lambda j: rw_copy(j, tile_source(j)).wait_recv())
+    each_tile(lambda j: rw_copy(j, tile_source(j)).wait_recv())
 
     def place(local, t):
         band_row = lax.broadcasted_iota(jnp.int32, (lmax, total_rows), 0)
@@ -186,14 +198,13 @@
 
     def step(s):
         c, local = lax.rem(s, chunks), lax.div(s, chunks)
-        each(n_proj, 1, lambda j: raw_copy(s, j, me_p).wait_send())
 
         @pl.when(s + DEPTH < steps)
         def _():
-            each(n_proj, 1, lambda j: raw_copy(s + DEPTH, j, me_p).start())
+            each_proj(lambda j: raw_copy(s + DEPTH, j, me_p).start())
 
         own_copy(s).wait()
-        each(n_proj, 1, lambda j: raw_copy(s, j, proj_peer(j)).wait_recv())
+        each_proj(lambda j: raw_copy(s, j, proj_peer(j)).wait_recv())
 
         def weigh(b):
             at = pl.ds(pl.multiple_of(b * 128, 128), 128)
@@ -209,13 +220,14 @@
 
         y = jnp.dot(wide[local], weighted[...], preferred_element_type=jnp.float32)
         ybuf[s] = y.astype(jnp.bfloat16).reshape(n_tile, slices, cw)
-        each(n_tile, 1, lambda j: z_copy(s, j, me_t).start())
+        each_tile(lambda j: z_copy(s, j, me_t).start())
         column = pl.multiple_of(128 + me_t * cols_dev + c * cw, 128)
         zbuf[local, :, pl.ds(column, cw)] = ybuf[s, me_t]
+        each_proj(lambda j: raw_copy(s, j, me_p).wait_send())
 
     def window(local):
         def arrived(s):
-            each(n_tile, 1, lambda j: z_copy(s, j, tile_source(j)).wait_recv())
+            each_tile(lambda j: z_copy(s, j, tile_source(j)).wait_recv())
 
         each((local + 1) * chunks, local * chunks, arrived)
         part = zbuf[local]
@@ -278,20 +290,20 @@
             psend[n, :, :, 256 * half : 256 * half + 256] = value.reshape(
                 n_proj, slices // n_proj, 256
             ).astype(psend.dtype)
-        each(n_proj, 1, lambda j: p_copy(n, j, me_p).start())
+        each_proj(lambda j: p_copy(n, j, me_p).start())
         precv[n, me_p] = psend[n, me_p]
 
+    each_tile(lambda j: rw_copy(j, me_t).wait_send())
+    each_tile(lambda j: each(steps, 0, lambda s: z_copy(s, j, me_t).wait_send()))
     for n in range(PARTS):
-        each(n_proj, 1, lambda j: p_copy(n, j, proj_peer(j)).wait_recv())
+        each_proj(lambda j: p_copy(n, j, proj_peer(j)).wait_recv())
         total = precv[n, 0].astype(jnp.float32)
         for source in range(1, n_proj):
             total = total + precv[n, source].astype(jnp.float32)
         out[:, n * part_cols : (n + 1) * part_cols] = total
 
-    each(n_tile, 1, lambda j: rw_copy(j, me_t).wait_send())
-    each(n_tile, 1, lambda j: each(steps, 0, lambda s: z_copy(s, j, me_t).wait_send()))
     for n in range(PARTS):
-        each(n_proj, 1, lambda j: p_copy(n, j, me_p).wait_send())
+        each_proj(lambda j: p_copy(n, j, me_p).wait_send())
 
 
 def body(raw, row_weights, col_weights, band_start, band_length, col_offset):

time: 80.6 us -> 75.7 us (0.939)
  Pallas kernels: 78.9 us -> 73.9 us
    pallas_call x1, Pallas kernels: 78.9 us -> 73.9 us  [body(): pl.pallas_call(functools.partial(kernel, n_proj, n_tile, chunks, cw), out...]
where the time goes in v5:
time: 75.7 us; the launch traced here: 75.5 us
  Pallas kernels  73.9 us (98%)
  local copies, waits for them, and re-layouts  1.57 us (2%)
    pallas_call x1, Pallas kernels, body(): pl.pallas_call(functools.partial(kernel, n_proj, n_tile, chunks, cw), out...  73.9 us
    unnamed x1, local copies, waits for them, and re-layouts  1.57 us

profile of v5, /device:TPU:0, one launch (start us, length us, event | category | flops | bytes accessed | tf_op | source)
XLA Modules:
  0.0 75.5 jit_solution(336580434057289466)
XLA Ops:
  0.0 73.9 %shard_map.64 = f32[16,2048]{1,0:T(8,128)} custom-call(s32[4,16]{1,0:T(4,128)} %bitcast.3, s32[4,16]{1,0:T(4,128)} %bitcast.4, s32[1,2]{1,0:T(1,128)} %bitcast.5, bf16[2,1,128,256]{3,2,1,0:T(8,128)(2,1)} %rw.1, bf16[16,128,1024]{2,1,0:T(8,128)(2,1)} %raw.1, bf16[2,1,1024,2048]{3,2,1,0:T(8,128)(2,1)} %col_w.1), custom_call_target="tpu_custom_call" | custom-call | flops 2147483648 | bytes 16777216 | tf_op jit(solution)/shard_map/pallas_call | solution.py:327
  74.0 1.6 %copy.8 = f32[16,2048]{1,0:T(8,128)} copy(f32[16,2048]{1,0:T(8,128)} %shard_map.64) | data formatting | bytes 262144

commit v6 on v5

--- a/solution.py
+++ b/solution.py
@@ -9,9 +9,9 @@
 from jax.sharding import PartitionSpec as P
 
 MESH = pl.DeviceIdType.MESH
-CHUNK = 256
+CHUNK = 128
 PARTS = 4
-DEPTH = 3
+DEPTH = 6
 VMEM_BYTES = 63 * 1024 * 1024
 
 
@@ -269,7 +269,7 @@
         for t in range(n_tile):
             place(local, t)
         if local > 0:
-            until = min(local * chunks + 2, steps)
+            until = min(local * chunks + (chunks + 1) // 2, steps)
             each(until, done, step)
             done = until
             add_up(local - 1)

time: 75.7 us -> 77.4 us (1.022)
  Pallas kernels: 73.9 us -> 75.7 us
    pallas_call x1, Pallas kernels: 73.9 us -> 75.7 us  [body(): pl.pallas_call(functools.partial(kernel, n_proj, n_tile, chunks, cw), out...]
where the time goes in v6:
time: 77.4 us; the launch traced here: 77.3 us
  Pallas kernels  75.7 us (98%)
  local copies, waits for them, and re-layouts  1.57 us (2%)
    pallas_call x1, Pallas kernels, body(): pl.pallas_call(functools.partial(kernel, n_proj, n_tile, chunks, cw), out...  75.7 us
    unnamed x1, local copies, waits for them, and re-layouts  1.57 us

profile of v6, /device:TPU:0, one launch (start us, length us, event | category | flops | bytes accessed | tf_op | source)
XLA Modules:
  0.0 77.3 jit_solution(5363386320850343365)
XLA Ops:
  0.0 75.7 %shard_map.64 = f32[16,2048]{1,0:T(8,128)} custom-call(s32[4,16]{1,0:T(4,128)} %bitcast.3, s32[4,16]{1,0:T(4,128)} %bitcast.4, s32[1,2]{1,0:T(1,128)} %bitcast.5, bf16[2,1,128,256]{3,2,1,0:T(8,128)(2,1)} %rw.1, bf16[16,128,1024]{2,1,0:T(8,128)(2,1)} %raw.1, bf16[2,1,1024,2048]{3,2,1,0:T(8,128)(2,1)} %col_w.1), custom_call_target="tpu_custom_call" | custom-call | flops 2147483648 | bytes 16777216 | tf_op jit(solution)/shard_map/pallas_call | solution.py:327
  75.7 1.6 %copy.8 = f32[16,2048]{1,0:T(8,128)} copy(f32[16,2048]{1,0:T(8,128)} %shard_map.64) | data formatting | bytes 262144

commit v7 on v5

--- a/solution.py
+++ b/solution.py
@@ -203,20 +203,21 @@
         def _():
             each_proj(lambda j: raw_copy(s + DEPTH, j, me_p).start())
 
-        own_copy(s).wait()
-        each_proj(lambda j: raw_copy(s, j, proj_peer(j)).wait_recv())
-
-        def weigh(b):
-            at = pl.ds(pl.multiple_of(b * 128, 128), 128)
-            row = b * 128 + lax.broadcasted_iota(jnp.int32, (128, cw), 0)
-            column = me_t * cols_dev + c * cw + lax.broadcasted_iota(jnp.int32, (128, cw), 1)
+        def weigh(source):
+            at = pl.ds(pl.multiple_of(source * rows_dev, rows_dev), rows_dev)
+            row = source * rows_dev + lax.broadcasted_iota(jnp.int32, (rows_dev, cw), 0)
+            column = me_t * cols_dev + c * cw + lax.broadcasted_iota(jnp.int32, (rows_dev, cw), 1)
             v = row.astype(jnp.float32) + (0.5 - total_rows / 2.0)
             u = column.astype(jnp.float32) + (0.5 - total_cols / 2.0)
             weight = dist * lax.rsqrt(dist * dist + u * u + v * v)
             value = landing[c, local, at, :].astype(jnp.float32) * weight
             weighted[at, :] = value.astype(jnp.bfloat16)
 
-        each(total_rows // 128, 0, weigh)
+        own_copy(s).wait()
+        weigh(me_p)
+        for j in proj_peers:
+            raw_copy(s, j, proj_peer(j)).wait_recv()
+            weigh(proj_peer(j))
 
         y = jnp.dot(wide[local], weighted[...], preferred_element_type=jnp.float32)
         ybuf[s] = y.astype(jnp.bfloat16).reshape(n_tile, slices, cw)

time: 75.7 us -> 75.4 us (level)
  no operation moved by 1% of the time
where the time goes in v7:
time: 75.4 us; the launch traced here: 75.3 us
  Pallas kernels  73.7 us (98%)
  local copies, waits for them, and re-layouts  1.57 us (2%)
    pallas_call x1, Pallas kernels, body(): pl.pallas_call(functools.partial(kernel, n_proj, n_tile, chunks, cw), out...  73.7 us
    unnamed x1, local copies, waits for them, and re-layouts  1.57 us

profile of v7, /device:TPU:0, one launch (start us, length us, event | category | flops | bytes accessed | tf_op | source)
XLA Modules:
  0.0 75.3 jit_solution(2109943278292952079)
XLA Ops:
  0.0 73.7 %shard_map.64 = f32[16,2048]{1,0:T(8,128)} custom-call(s32[4,16]{1,0:T(4,128)} %bitcast.3, s32[4,16]{1,0:T(4,128)} %bitcast.4, s32[1,2]{1,0:T(1,128)} %bitcast.5, bf16[2,1,128,256]{3,2,1,0:T(8,128)(2,1)} %rw.1, bf16[16,128,1024]{2,1,0:T(8,128)(2,1)} %raw.1, bf16[2,1,1024,2048]{3,2,1,0:T(8,128)(2,1)} %col_w.1), custom_call_target="tpu_custom_call" | custom-call | flops 2147483648 | bytes 16777216 | tf_op jit(solution)/shard_map/pallas_call | solution.py:328
  73.7 1.6 %copy.8 = f32[16,2048]{1,0:T(8,128)} copy(f32[16,2048]{1,0:T(8,128)} %shard_map.64) | data formatting | bytes 262144
